TPU v7x, 32 devices: a whole 2x2x4 slice. The times are simulated.
32 devices in a mesh: site: 4 (over y, core), blk: 8 (over z, x).
Axes of the slice: x: 2, y: 2, z: 4, core: 2. Of those that a mesh axis runs over, the one named last changes fastest.
Arguments:
- corner: bfloat16 [4, 48, 128, 128], P('site', 'blk')
- bcorner: bfloat16 [2, 4, 48, 128, 128], P(None, 'site', 'blk'), may hold values from -6 to 6
- edge: bfloat16 [4, 48, 128, 2304], P('site', 'blk'), may hold values from -0.5 to 0.5
- bedge: bfloat16 [4, 48, 128, 2304], P('site', 'blk'), may hold values from -0.5 to 0.5
- proj: bfloat16 [4, 48, 2304, 128], P('site', 'blk'), may hold values from -0.125 to 0.125
- joining: int32 [4, 48], P('site'), may hold values from 0 to 47, as said below
- momentum: float32 [1], replicated, may hold values from 0.5 to 2.5
Outputs:
- new_corner: bfloat16 [4, 48, 128, 128], P('site', 'blk')
- new_bcorner: bfloat16 [2, 4, 48, 128, 128], P(None, 'site', 'blk')
- momentum_sum: float32 [2, 48, 128, 128], P(None, 'blk', 'site')
Inputs may be any that keep to these rules, and one draw needn't show every extreme that they name: Each row of joining is a permutation of the 48 slots. The 6 new slots of one blk device take their blocks from the slots of at most 3 blk devices, exactly 2 from each of them.
All inputs are finite; a program needn't handle non-finite values. Where the computation divides by a largest or mean magnitude, that divisor is 1e-20 or more.
Results may differ from a plain program's by a relative error of at most 0.024.
Values may be sent and summed in bfloat16 or wider, within the bound.
No kernel may reach another device: no remote copies, remote signals or barrier semaphores. Data moves between devices by JAX's collectives and lax.ppermute only.
A program may use at most 128 MiB of HBM per device.

v0:
```python
import functools

import jax
import jax.numpy as jnp
from jax import lax
from jax.experimental import pallas as pl
from jax.experimental.pallas import tpu as pltpu
from jax.sharding import PartitionSpec as P

epsilon = 1e-06
TILE = 16
VMEM = pl.BlockSpec(memory_space=pltpu.VMEM)
SMEM = pl.BlockSpec(memory_space=pltpu.SMEM)
HBM = pl.BlockSpec(memory_space=pltpu.HBM)


def all_swapped(parts, axis):
    n = len(parts)
    out = {k: lax.ppermute(parts[k], axis, [(i, i ^ k) for i in range(n)]) for k in range(n - 1, 0, -1)}
    return [parts[0]] + [out[k] for k in range(1, n)]


def edge_proj_kernel(edge, bedge, proj, wv_ref, edge_buf, bedge_buf, proj_buf, sems):
    slots = proj.shape[1]
    pairs = ((proj, proj_buf), (edge, edge_buf), (bedge, bedge_buf))
    copies = [
        [pltpu.make_async_copy(src.at[0, i], buf.at[i], sems.at[3 * i + a]) for a, (src, buf) in enumerate(pairs)]
        for i in range(slots)
    ]
    for group in copies:
        for copy in group:
            copy.start()
    dot = functools.partial(jnp.dot, preferred_element_type=jnp.float32)
    for i, (first, second, third) in enumerate(copies):
        first.wait()
        second.wait()
        wv_ref[2 * i] = dot(edge_buf[i], proj_buf[i]).astype(wv_ref.dtype)
        third.wait()
        wv_ref[2 * i + 1] = dot(bedge_buf[i], proj_buf[i]).astype(wv_ref.dtype)


def edge_proj(edge, bedge, proj):
    _, slots, m, k = edge.shape
    return pl.pallas_call(
        edge_proj_kernel,
        out_shape=jax.ShapeDtypeStruct((2 * slots, m, m), jnp.bfloat16),
        in_specs=[HBM] * 3,
        out_specs=VMEM,
        scratch_shapes=[
            pltpu.VMEM((slots, m, k), jnp.bfloat16),
            pltpu.VMEM((slots, m, k), jnp.bfloat16),
            pltpu.VMEM((slots, k, m), jnp.bfloat16),
            pltpu.SemaphoreType.DMA((3 * slots,)),
        ],
        cost_estimate=pl.CostEstimate(
            flops=4 * slots * m * k * m, bytes_accessed=6 * slots * m * k, transcendentals=0
        ),
        compiler_params=pltpu.CompilerParams(vmem_limit_bytes=60 << 20),
        name="edge_proj",
    )(edge, bedge, proj)


def small_call(kernel, out_shape, in_specs, scratch, name):
    return pl.pallas_call(
        kernel,
        out_shape=out_shape,
        in_specs=in_specs,
        out_specs=jax.tree.map(lambda _: VMEM, out_shape),
        scratch_shapes=scratch,
        cost_estimate=pl.CostEstimate(flops=1 << 28, bytes_accessed=1 << 20, transcendentals=0),
        compiler_params=pltpu.CompilerParams(vmem_limit_bytes=24 << 20),
        name=name,
    )


def blocks_of(turn, corner, bcorner, w, v):
    cosine, sine = turn
    dot = functools.partial(jnp.dot, preferred_element_type=jnp.float32)
    ground = dot(corner, w).astype(jnp.bfloat16)
    real_term = dot(bcorner[0], w)
    imag_term = dot(bcorner[1], w)
    re = cosine * real_term - sine * imag_term + dot(corner, v)
    im = sine * real_term + cosine * imag_term
    return ground, re.astype(jnp.bfloat16), im.astype(jnp.bfloat16)


def spread_kernel(n, here, turn, corner, bcorner, wv, *refs):
    out, stage = refs[:n], refs[n]
    slots, m = corner.shape[1], corner.shape[2]
    rows = m // n
    top = jnp.zeros((m, m), jnp.float32)
    for i in range(slots):
        b_here = (bcorner[0, 0, i], bcorner[1, 0, i])
        blocks = blocks_of((turn[0], turn[1]), corner[0, i], b_here, wv[2 * i], wv[2 * i + 1])
        top = jnp.maximum(top, jnp.abs(blocks[0].astype(jnp.float32)))
        for kind in range(3):
            stage[3 * i + kind] = blocks[kind]
    peak = jnp.full((TILE, m), jnp.max(top), jnp.float32).astype(jnp.bfloat16)
    for k in range(n):
        first = pl.multiple_of(jnp.bitwise_xor(here[0], k) * rows, rows)
        for b in range(3 * slots):
            out[k][b * rows : (b + 1) * rows] = stage[b, pl.ds(first, rows)]
        out[k][3 * slots * rows :] = peak


def route_kernel(n, slots, here, joining, *refs):
    pieces, out, held = refs[:n], refs[n : 2 * n], refs[2 * n]
    size = held.shape[1]
    for k in range(n):
        d = jnp.bitwise_xor(here[0], k)
        for i in range(slots):
            held[d * slots + i] = pieces[k][i * size : (i + 1) * size]
    top = functools.reduce(jnp.maximum, [piece[slots * size :].astype(jnp.float32) for piece in pieces])
    divisor = jnp.concatenate([top] * (size // TILE), axis=0) + epsilon
    for k in range(n):
        t = jnp.bitwise_xor(here[0], k)
        for i in range(slots):
            q = joining[0, t * slots + i]
            out[k][i * size : (i + 1) * size] = (held[q].astype(jnp.float32) / divisor).astype(jnp.bfloat16)


def share_kernel(n, sites, here, *refs):
    pieces, shares, stage = refs[:n], refs[n : n + sites], refs[n + sites]
    _, slots, wide, m = shares[0].shape
    rows = m // n
    for k in range(n):
        first = pl.multiple_of(jnp.bitwise_xor(here[0], k) * rows, rows)
        for i in range(slots):
            for c in range(2):
                at = (3 * i + 1 + c) * rows
                stage[c, i, pl.ds(first, rows)] = pieces[k][at : at + rows]
    for k in range(sites):
        first = pl.multiple_of(jnp.bitwise_xor(here[1], k) * wide, wide)
        for i in range(slots):
            for c in range(2):
                shares[k][c, i] = stage[c, i, pl.ds(first, wide)]


def join_kernel(n, here, *refs):
    pieces, new_corner, new_b = refs[:n], refs[n], refs[n + 1]
    _, slots, m, _ = new_corner.shape
    rows = m // n
    for k in range(n):
        first = pl.multiple_of(jnp.bitwise_xor(here[0], k) * rows, rows)
        for i in range(slots):
            at = 3 * i * rows
            new_corner[0, i, pl.ds(first, rows)] = pieces[k][at : at + rows]
            for c in range(2):
                at = (3 * i + 1 + c) * rows
                new_b[c, 0, i, pl.ds(first, rows)] = pieces[k][at : at + rows]


def routed_by_tiles(turn, corner, bcorner, wv, joining, n, sites):
    _, slots, m, _ = corner.shape
    rows = m // n
    shape = lambda *dims: jax.ShapeDtypeStruct(dims, jnp.bfloat16)
    scratch = lambda *dims: [pltpu.VMEM(dims, jnp.bfloat16)]
    bind = functools.partial
    here = jnp.stack([lax.axis_index("blk"), lax.axis_index("site")]).astype(jnp.int32)
    pieces = [shape(3 * slots * rows + TILE, m)] * n
    kept = scratch(3 * slots, m, m)
    parts = small_call(bind(spread_kernel, n), pieces, [SMEM] * 2 + [VMEM] * 3, kept, "spread")(
        here, turn, corner, bcorner, wv
    )
    parts = all_swapped(parts, "blk")
    pieces = [shape(3 * slots * rows, m)] * n
    kept = scratch(n * slots, 3 * rows, m)
    parts = small_call(bind(route_kernel, n, slots), pieces, [SMEM] * 2 + [VMEM] * n, kept, "route")(
        here, joining, *parts
    )
    parts = all_swapped(parts, "blk")
    ins = [SMEM] + [VMEM] * n
    pieces = [shape(2, slots, m // sites, m)] * sites
    shares = small_call(bind(share_kernel, n, sites), pieces, ins, scratch(2, slots, m, m), "share")(here, *parts)
    shares = all_swapped(shares, "site")
    pieces = [shape(1, slots, m, m), shape(2, 1, slots, m, m)]
    new_corner, new_b = small_call(bind(join_kernel, n), pieces, ins, [], "join")(here, *parts)
    return new_corner, new_b, shares


def transposed(pieces):
    return lax.all_to_all(pieces, "blk", 0, 0, tiled=True)


def routed_by_rows(turn, corner, bcorner, wv, joining, n, sites):
    _, slots, m, _ = corner.shape
    rows = m // n
    wv = wv.reshape(slots, 2, m, m)
    ground, re, im = jax.vmap(lambda c, b, x: blocks_of((turn[0], turn[1]), c, b, x[0], x[1]))(
        corner[0], jnp.moveaxis(bcorner[:, 0], 0, 1), wv
    )
    peak = lax.pmax(jnp.max(jnp.abs(ground)).astype(jnp.float32), "blk")
    blocks = jnp.moveaxis(jnp.stack([ground, re, im], axis=1).reshape(slots, 3, n, rows, m), 2, 0)
    pieces = transposed(blocks).reshape(n * slots, 3, rows, m)
    scaled = (pieces[joining[0]].astype(jnp.float32) / (peak + epsilon)).astype(jnp.bfloat16)
    final = transposed(scaled.reshape(n, slots, 3, rows, m))
    new = jnp.transpose(final, (2, 1, 0, 3, 4)).reshape(3, slots, m, m)
    shares = jnp.moveaxis(new[1:].reshape(2, slots, sites, m // sites, m), 2, 0)
    shares = lax.all_to_all(shares, "site", 0, 0, tiled=True)
    return new[0][None], new[1:][:, None], [shares[i] for i in range(sites)]


def per_device(corner, bcorner, edge, bedge, proj, joining, momentum):
    m = corner.shape[2]
    n, sites = lax.axis_size("blk"), lax.axis_size("site")
    angle = momentum[0] * lax.axis_index("site").astype(jnp.float32)
    turn = jnp.stack([jnp.cos(angle), jnp.sin(angle)])
    onward = [(i, (i + 1) % sites) for i in range(sites)]
    left_corner = lax.ppermute(corner, "site", onward)
    left_bcorner = lax.ppermute(bcorner, "site", onward)
    wv = edge_proj(edge, bedge, proj)
    routed = routed_by_tiles if m % (n * TILE) == 0 and m % (sites * TILE) == 0 else routed_by_rows
    new_corner, new_b, shares = routed(turn, left_corner, left_bcorner, wv, joining, n, sites)
    summed = shares[0].astype(jnp.float32)
    for share in shares[1:]:
        summed = summed + share.astype(jnp.float32)
    return (new_corner, new_b, summed)


def solution(mesh):
    in_specs = (
        P("site", "blk", None, None),
        P(None, "site", "blk", None, None),
        P("site", "blk", None, None),
        P("site", "blk", None, None),
        P("site", "blk", None, None),
        P("site", None),
        P(),
    )
    out_specs = (
        P("site", "blk", None, None),
        P(None, "site", "blk", None, None),
        P(None, "blk", "site", None),
    )
    return jax.shard_map(
        per_device, mesh=mesh, in_specs=in_specs, out_specs=out_specs, check_vma=False
    )
```

profile of v0, /device:TPU:0, one launch (start us, length us, event | category | flops | bytes accessed | tf_op | source)
XLA Modules:
  0.0 59.0 jit_solution(18091459005679117707)
XLA Ops:
  0.6 0.5 collective-permute-start.1
  1.1 2.6 %collective-permute-start = (bf16[1,6,128,128]{3,2,1,0:T(8,128)(2,1)}, bf16[1,6,128,128]{3,2,1,0:T(8,128)(2,1)S(1)}, u32[]{:S(2)}, u32[]{:S(2)}) collective-permute-start(bf16[1,6,128,128]{3,2,1,0:T(8,128)(2,1)} %param.7), channel_id=1, source_target_pairs={{0,8},{8,16},{16,24},{24,0},{1,9},{9,17},{17,25},{25,1},{2,10},{10... | collective-permute-start | bytes 589832 | tf_op jit(solution)/shard_map/ppermute | solution.py:209
  4.6 0.1 pad_add_fusion.here
  4.6 6.0 %edge_proj.1.wv = bf16[12,128,128]{2,1,0:T(8,128)(2,1)} custom-call(bf16[1,6,128,2304]{3,2,1,0:T(8,128)(2,1)} %edge.1, bf16[1,6,128,2304]{3,2,1,0:T(8,128)(2,1)} %bedge.1, bf16[1,6,2304,128]{3,2,1,0:T(8,128)(2,1)} %proj.1), custom_call_target="tpu_custom_call" | custom-call | flops 905969664 | bytes 10616832 | tf_op jit(solution)/shard_map/edge_proj/pallas_call | solution.py:44
  10.7 0.1 pad_maximum_fusion.turn
  10.8 0.1 collective-permute-done.corner
  10.9 0.0 collective-permute-done.1.bcorner
  10.9 1.0 %copy-done = bf16[12,128,128]{2,1,0:T(8,128)(2,1)S(1)} copy-done((bf16[12,128,128]{2,1,0:T(8,128)(2,1)S(1)}, bf16[12,128,128]{2,1,0:T(8,128)(2,1)}, u32[]{:S(2)}) %copy-start) | copy-done | bytes 393240
  11.9 1.0 %spread.1 = (bf16[304,128]{1,0:T(8,128)(2,1)S(1)}, bf16[304,128]{1,0:T(8,128)(2,1)S(1)}, bf16[304,128]{1,0:T(8,128)(2,1)S(1)}, bf16[304,128]{1,0:T(8,128)(2,1)S(...) custom-call(s32[2]{0:T(128)S(1)} %pad_add_fusion.here, ...), custom_call_target="tpu_custom_call" | custom-call | flops 268435456 | bytes 1048576 | tf_op jit(solution)/shard_map/spread/pallas_call | solution.py:162
  12.9 2.3 %collective-permute-start.2 = (bf16[304,128]{1,0:T(8,128)(2,1)S(1)}, bf16[304,128]{1,0:T(8,128)(2,1)S(1)}, u32[]{:S(2)}, u32[]{:S(2)}) collective-permute-start(bf16[304,128]{1,0:T(8,128)(2,1)S(1)} %get-tuple-element.26), channel_id=1, source_target_pairs={{0,1},{1,0},{2,3},{3,2},{4,5},{5,4},{6,7},{7,6},{8,9},{9,8},{10,11... | collective-permute-start | bytes 233480 | tf_op jit(solution)/shard_map/ppermute | solution.py:19
  15.2 1.6 %collective-permute-start.3 = (bf16[304,128]{1,0:T(8,128)(2,1)S(1)}, bf16[304,128]{1,0:T(8,128)(2,1)S(1)}, u32[]{:S(2)}, u32[]{:S(2)}) collective-permute-start(bf16[304,128]{1,0:T(8,128)(2,1)S(1)} %get-tuple-element.27), channel_id=1, source_target_pairs={{0,2},{1,3},{2,0},{3,1},{4,6},{5,7},{6,4},{7,5},{8,10},{9,11},{10,... | collective-permute-start | bytes 233480 | tf_op jit(solution)/shard_map/ppermute | solution.py:19
  16.8 0.0 collective-permute-start.4
  16.8 3.0 %collective-permute-start.5 = (bf16[304,128]{1,0:T(8,128)(2,1)S(1)}, bf16[304,128]{1,0:T(8,128)(2,1)S(1)}, u32[]{:S(2)}, u32[]{:S(2)}) collective-permute-start(bf16[304,128]{1,0:T(8,128)(2,1)S(1)} %get-tuple-element.29), channel_id=1, source_target_pairs={{0,4},{1,5},{2,6},{3,7},{4,0},{5,1},{6,2},{7,3},{8,12},{9,13},{10,... | collective-permute-start | bytes 233480 | tf_op jit(solution)/shard_map/ppermute | solution.py:19
  19.8 1.3 %collective-permute-start.6 = (bf16[304,128]{1,0:T(8,128)(2,1)S(1)}, bf16[304,128]{1,0:T(8,128)(2,1)S(1)}, u32[]{:S(2)}, u32[]{:S(2)}) collective-permute-start(bf16[304,128]{1,0:T(8,128)(2,1)S(1)} %get-tuple-element.30), channel_id=1, source_target_pairs={{0,5},{1,4},{2,7},{3,6},{4,1},{5,0},{6,3},{7,2},{8,13},{9,12},{10,... | collective-permute-start | bytes 233480 | tf_op jit(solution)/shard_map/ppermute | solution.py:19
  21.1 0.0 collective-permute-done.2.refs_1_
  21.1 3.6 %collective-permute-start.7 = (bf16[304,128]{1,0:T(8,128)(2,1)S(1)}, bf16[304,128]{1,0:T(8,128)(2,1)S(1)}, u32[]{:S(2)}, u32[]{:S(2)}) collective-permute-start(bf16[304,128]{1,0:T(8,128)(2,1)S(1)} %get-tuple-element.31), channel_id=1, source_target_pairs={{0,6},{1,7},{2,4},{3,5},{4,2},{5,3},{6,0},{7,1},{8,14},{9,15},{10,... | collective-permute-start | bytes 233480 | tf_op jit(solution)/shard_map/ppermute | solution.py:19
  24.7 0.0 collective-permute-done.3.refs_2_
  24.7 0.0 collective-permute-start.8
  24.7 0.0 collective-permute-done.4.refs_3_
  24.7 0.0 collective-permute-done.5.refs_4_
  24.7 7.8 %collective-permute-done.6.refs_5_ = bf16[304,128]{1,0:T(8,128)(2,1)S(1)} collective-permute-done((bf16[304,128]{1,0:T(8,128)(2,1)S(1)}, bf16[304,128]{1,0:T(8,128)(2,1)S(1)}, u32[]{:S(2)}, u32[]{:S(2)}) %collective-permute-start.6) | collective-permute-done | bytes 77856 | tf_op jit(solution)/shard_map/ppermute | solution.py:19
  32.6 0.0 collective-permute-done.7.refs_6_
  32.6 0.0 collective-permute-done.8.refs_7_
  32.6 0.0 copy-done.1
  32.6 0.7 %route.1 = (bf16[288,128]{1,0:T(8,128)(2,1)S(1)}, bf16[288,128]{1,0:T(8,128)(2,1)S(1)}, bf16[288,128]{1,0:T(8,128)(2,1)S(1)}, bf16[288,128]{1,0:T(8,128)(2,1)S(1...) custom-call(s32[2]{0:T(128)S(1)} %pad_add_fusion.here, ...), custom_call_target="tpu_custom_call" | custom-call | flops 268435456 | bytes 1048576 | tf_op jit(solution)/shard_map/route/pallas_call | solution.py:168
  33.3 0.1 collective-permute-start.9
  33.4 3.2 %collective-permute-start.10 = (bf16[288,128]{1,0:T(8,128)(2,1)S(1)}, bf16[288,128]{1,0:T(8,128)(2,1)S(1)}, u32[]{:S(2)}, u32[]{:S(2)}) collective-permute-start(bf16[288,128]{1,0:T(8,128)(2,1)S(1)} %get-tuple-element.35), channel_id=1, source_target_pairs={{0,2},{1,3},{2,0},{3,1},{4,6},{5,7},{6,4},{7,5},{8,10},{9,11},{10,... | collective-permute-start | bytes 221192 | tf_op jit(solution)/shard_map/ppermute | solution.py:19
  36.5 1.1 %collective-permute-start.11 = (bf16[288,128]{1,0:T(8,128)(2,1)S(1)}, bf16[288,128]{1,0:T(8,128)(2,1)S(1)}, u32[]{:S(2)}, u32[]{:S(2)}) collective-permute-start(bf16[288,128]{1,0:T(8,128)(2,1)S(1)} %get-tuple-element.36), channel_id=1, source_target_pairs={{0,3},{1,2},{2,1},{3,0},{4,7},{5,6},{6,5},{7,4},{8,11},{9,10},{10,... | collective-permute-start | bytes 221192 | tf_op jit(solution)/shard_map/ppermute | solution.py:19
  37.6 2.7 %collective-permute-start.12 = (bf16[288,128]{1,0:T(8,128)(2,1)S(1)}, bf16[288,128]{1,0:T(8,128)(2,1)S(1)}, u32[]{:S(2)}, u32[]{:S(2)}) collective-permute-start(bf16[288,128]{1,0:T(8,128)(2,1)S(1)} %get-tuple-element.37), channel_id=1, source_target_pairs={{0,4},{1,5},{2,6},{3,7},{4,0},{5,1},{6,2},{7,3},{8,12},{9,13},{10,... | collective-permute-start | bytes 221192 | tf_op jit(solution)/shard_map/ppermute | solution.py:19
  40.3 0.3 collective-permute-start.13
  40.6 0.0 collective-permute-done.9.refs_1_
  40.6 2.1 %collective-permute-start.14 = (bf16[288,128]{1,0:T(8,128)(2,1)S(1)}, bf16[288,128]{1,0:T(8,128)(2,1)S(1)}, u32[]{:S(2)}, u32[]{:S(2)}) collective-permute-start(bf16[288,128]{1,0:T(8,128)(2,1)S(1)} %get-tuple-element.39), channel_id=1, source_target_pairs={{0,6},{1,7},{2,4},{3,5},{4,2},{5,3},{6,0},{7,1},{8,14},{9,15},{10,... | collective-permute-start | bytes 221192 | tf_op jit(solution)/shard_map/ppermute | solution.py:19
  42.7 0.0 collective-permute-done.10.refs_2_
  42.7 2.6 %collective-permute-start.15 = (bf16[288,128]{1,0:T(8,128)(2,1)S(1)}, bf16[288,128]{1,0:T(8,128)(2,1)S(1)}, u32[]{:S(2)}, u32[]{:S(2)}) collective-permute-start(bf16[288,128]{1,0:T(8,128)(2,1)S(1)} %get-tuple-element.40), channel_id=1, source_target_pairs={{0,7},{1,6},{2,5},{3,4},{4,3},{5,2},{6,1},{7,0},{8,15},{9,14},{10,... | collective-permute-start | bytes 221192 | tf_op jit(solution)/shard_map/ppermute | solution.py:19
  45.3 0.0 collective-permute-done.11.refs_3_
  45.3 3.1 %collective-permute-done.12.refs_4_ = bf16[288,128]{1,0:T(8,128)(2,1)S(1)} collective-permute-done((bf16[288,128]{1,0:T(8,128)(2,1)S(1)}, bf16[288,128]{1,0:T(8,128)(2,1)S(1)}, u32[]{:S(2)}, u32[]{:S(2)}) %collective-permute-start.12) | collective-permute-done | bytes 73760 | tf_op jit(solution)/shard_map/ppermute | solution.py:19
  48.4 2.3 %collective-permute-done.13.refs_5_ = bf16[288,128]{1,0:T(8,128)(2,1)S(1)} collective-permute-done((bf16[288,128]{1,0:T(8,128)(2,1)S(1)}, bf16[288,128]{1,0:T(8,128)(2,1)S(1)}, u32[]{:S(2)}, u32[]{:S(2)}) %collective-permute-start.13) | collective-permute-done | bytes 73760 | tf_op jit(solution)/shard_map/ppermute | solution.py:19
  50.7 0.0 collective-permute-done.14.refs_6_
  50.7 0.0 collective-permute-done.15.refs_7_
  50.7 0.6 %share.1 = (bf16[2,6,32,128]{3,2,1,0:T(8,128)(2,1)S(1)}, bf16[2,6,32,128]{3,2,1,0:T(8,128)(2,1)S(1)}, bf16[2,6,32,128]{3,2,1,0:T(8,128)(2,1)S(1)}, bf16[2,6,32,128]{3,2,1,0:T(8,128)(2,1)S(1)}) custom-call(s32[2]{0:T(128)S(1)} %pad_add_fusion.here, bf16[288,128]{1,0:T(8,128)(2,1)S(1)} %get-tuple-element.33.refs_0_, ...), custom_call_target="tpu_custom_call" | custom-call | flops 268435456 | bytes 1048576 | tf_op jit(solution)/shard_map/share/pallas_call | solution.py:174
  51.3 0.1 collective-permute-start.16
  51.4 0.4 collective-permute-start.17
  51.8 1.5 %collective-permute-start.18 = (bf16[2,6,32,128]{3,2,1,0:T(8,128)(2,1)S(1)}, bf16[2,6,32,128]{3,2,1,0:T(8,128)(2,1)S(1)}, u32[]{:S(2)}, u32[]{:S(2)}) collective-permute-start(bf16[2,6,32,128]{3,2,1,0:T(8,128)(2,1)S(1)} %get-tuple-element.46), channel_id=1, source_target_pairs={{0,24},{8,16},{16,8},{24,0},{1,25},{9,17},{17,9},{25,1},{2,26},{10... | collective-permute-start | bytes 294920 | tf_op jit(solution)/shard_map/ppermute | solution.py:19
  53.2 1.4 %join.1 = (bf16[1,6,128,128]{3,2,1,0:T(8,128)(2,1)}, bf16[2,1,6,128,128]{4,3,2,1,0:T(8,128)(2,1)}) custom-call(s32[2]{0:T(128)S(1)} %pad_add_fusion.here, bf16[288,128]{1,0:T(8,128)(2,1)S(1)} %get-tuple-element.33.refs_0_, bf16[288,128]{1,0:T(8,128)(2,1)S(1)} %collective-permute-done.9.refs_1_, bf16[288,128]{1,0:T(8,128)(2,1)S(1)} %collective-permute-done.10.refs_2_, ...), custom_call_target="tpu_custom_call" | custom-call | flops 268435456 | bytes 1048576 | tf_op jit(solution)/shard_map/join/pallas_call | solution.py:177
  54.6 0.0 collective-permute-done.16
  54.7 2.4 %collective-permute-done.17 = bf16[2,6,32,128]{3,2,1,0:T(8,128)(2,1)S(1)} collective-permute-done((bf16[2,6,32,128]{3,2,1,0:T(8,128)(2,1)S(1)}, bf16[2,6,32,128]{3,2,1,0:T(8,128)(2,1)S(1)}, u32[]{:S(2)}, u32[]{:S(2)}) %collective-permute-start.17) | collective-permute-done | bytes 98336 | tf_op jit(solution)/shard_map/ppermute | solution.py:19
  57.0 1.2 %collective-permute-done.18 = bf16[2,6,32,128]{3,2,1,0:T(8,128)(2,1)S(1)} collective-permute-done((bf16[2,6,32,128]{3,2,1,0:T(8,128)(2,1)S(1)}, bf16[2,6,32,128]{3,2,1,0:T(8,128)(2,1)S(1)}, u32[]{:S(2)}, u32[]{:S(2)}) %collective-permute-start.18) | collective-permute-done | bytes 98336 | tf_op jit(solution)/shard_map/ppermute | solution.py:19
  58.2 0.7 %convert_add_fusion = f32[2,6,32,128]{3,2,1,0:T(8,128)} fusion(bf16[2,6,32,128]{3,2,1,0:T(8,128)(2,1)S(1)} %collective-permute-done.18, bf16[2,6,32,128]{3,2,1,0:T(8,128)(2,1)S(1)} %collective-permute-done.17, bf16[2,6,32,128]{3,2,1,0:T(8,128)(2,1)S(1)} %collective-permute-done.16, bf16[2,6,32,128]{3,2,1,0:T(8,128)(2,1)S(1)} %get-tuple-element.43), kind=kLoop, calls=%fused_computation | loop fusion | flops 344064 | bytes 589824 | tf_op jit(solution)/shard_map/add | solution.py:216
  (2 shorter events, 0.0 us)
Async XLA Ops:
  0.6 10.2 %collective-permute-start.1 = (bf16[2,1,6,128,128]{4,3,2,1,0:T(8,128)(2,1)}, bf16[2,1,6,128,128]{4,3,2,1,0:T(8,128)(2,1)S(1)}, u32[]{:S(2)}, u32[]{:S(2)}) collective-permute-start(bf16[2,1,6,128,128]{4,3,2,1,0:T(8,128)(2,1)} %param.8), channel_id=1, source_target_pairs={{0,8},{8,16},{16,24},{24,0},{1,9},{9,17},{17,25},{25,1},{2,10},{10... | collective-permute-start | bytes 1179656 | tf_op jit(solution)/shard_map/ppermute | solution.py:210
  1.1 9.7 %collective-permute-start = (bf16[1,6,128,128]{3,2,1,0:T(8,128)(2,1)}, bf16[1,6,128,128]{3,2,1,0:T(8,128)(2,1)S(1)}, u32[]{:S(2)}, u32[]{:S(2)}) collective-permute-start(bf16[1,6,128,128]{3,2,1,0:T(8,128)(2,1)} %param.7), channel_id=1, source_target_pairs={{0,8},{8,16},{16,24},{24,0},{1,9},{9,17},{17,25},{25,1},{2,10},{10... | collective-permute-start | bytes 589832 | tf_op jit(solution)/shard_map/ppermute | solution.py:209
  4.6 27.9 %copy-start.1 = (s32[1,48]{1,0:T(1,128)S(1)}, s32[1,48]{1,0:T(1,128)}, u32[]{:S(2)}) copy-start(s32[1,48]{1,0:T(1,128)} %joining.1) | copy-start | bytes 580
  10.9 1.0 %copy-start = (bf16[12,128,128]{2,1,0:T(8,128)(2,1)S(1)}, bf16[12,128,128]{2,1,0:T(8,128)(2,1)}, u32[]{:S(2)}) copy-start(bf16[12,128,128]{2,1,0:T(8,128)(2,1)} %edge_proj.1.wv) | copy-start | bytes 1179652
  12.9 8.2 %collective-permute-start.2 = (bf16[304,128]{1,0:T(8,128)(2,1)S(1)}, bf16[304,128]{1,0:T(8,128)(2,1)S(1)}, u32[]{:S(2)}, u32[]{:S(2)}) collective-permute-start(bf16[304,128]{1,0:T(8,128)(2,1)S(1)} %get-tuple-element.26), channel_id=1, source_target_pairs={{0,1},{1,0},{2,3},{3,2},{4,5},{5,4},{6,7},{7,6},{8,9},{9,8},{10,11... | collective-permute-start | bytes 233480 | tf_op jit(solution)/shard_map/ppermute | solution.py:19
  15.2 9.5 %collective-permute-start.3 = (bf16[304,128]{1,0:T(8,128)(2,1)S(1)}, bf16[304,128]{1,0:T(8,128)(2,1)S(1)}, u32[]{:S(2)}, u32[]{:S(2)}) collective-permute-start(bf16[304,128]{1,0:T(8,128)(2,1)S(1)} %get-tuple-element.27), channel_id=1, source_target_pairs={{0,2},{1,3},{2,0},{3,1},{4,6},{5,7},{6,4},{7,5},{8,10},{9,11},{10,... | collective-permute-start | bytes 233480 | tf_op jit(solution)/shard_map/ppermute | solution.py:19
  16.8 7.9 %collective-permute-start.4 = (bf16[304,128]{1,0:T(8,128)(2,1)S(1)}, bf16[304,128]{1,0:T(8,128)(2,1)S(1)}, u32[]{:S(2)}, u32[]{:S(2)}) collective-permute-start(bf16[304,128]{1,0:T(8,128)(2,1)S(1)} %get-tuple-element.28), channel_id=1, source_target_pairs={{0,3},{1,2},{2,1},{3,0},{4,7},{5,6},{6,5},{7,4},{8,11},{9,10},{10,... | collective-permute-start | bytes 233480 | tf_op jit(solution)/shard_map/ppermute | solution.py:19
  16.8 7.9 %collective-permute-start.5 = (bf16[304,128]{1,0:T(8,128)(2,1)S(1)}, bf16[304,128]{1,0:T(8,128)(2,1)S(1)}, u32[]{:S(2)}, u32[]{:S(2)}) collective-permute-start(bf16[304,128]{1,0:T(8,128)(2,1)S(1)} %get-tuple-element.29), channel_id=1, source_target_pairs={{0,4},{1,5},{2,6},{3,7},{4,0},{5,1},{6,2},{7,3},{8,12},{9,13},{10,... | collective-permute-start | bytes 233480 | tf_op jit(solution)/shard_map/ppermute | solution.py:19
  19.8 12.7 %collective-permute-start.6 = (bf16[304,128]{1,0:T(8,128)(2,1)S(1)}, bf16[304,128]{1,0:T(8,128)(2,1)S(1)}, u32[]{:S(2)}, u32[]{:S(2)}) collective-permute-start(bf16[304,128]{1,0:T(8,128)(2,1)S(1)} %get-tuple-element.30), channel_id=1, source_target_pairs={{0,5},{1,4},{2,7},{3,6},{4,1},{5,0},{6,3},{7,2},{8,13},{9,12},{10,... | collective-permute-start | bytes 233480 | tf_op jit(solution)/shard_map/ppermute | solution.py:19
  21.1 11.5 %collective-permute-start.7 = (bf16[304,128]{1,0:T(8,128)(2,1)S(1)}, bf16[304,128]{1,0:T(8,128)(2,1)S(1)}, u32[]{:S(2)}, u32[]{:S(2)}) collective-permute-start(bf16[304,128]{1,0:T(8,128)(2,1)S(1)} %get-tuple-element.31), channel_id=1, source_target_pairs={{0,6},{1,7},{2,4},{3,5},{4,2},{5,3},{6,0},{7,1},{8,14},{9,15},{10,... | collective-permute-start | bytes 233480 | tf_op jit(solution)/shard_map/ppermute | solution.py:19
  24.7 7.9 %collective-permute-start.8 = (bf16[304,128]{1,0:T(8,128)(2,1)S(1)}, bf16[304,128]{1,0:T(8,128)(2,1)S(1)}, u32[]{:S(2)}, u32[]{:S(2)}) collective-permute-start(bf16[304,128]{1,0:T(8,128)(2,1)S(1)} %get-tuple-element.32), channel_id=1, source_target_pairs={{0,7},{1,6},{2,5},{3,4},{4,3},{5,2},{6,1},{7,0},{8,15},{9,14},{10,... | collective-permute-start | bytes 233480 | tf_op jit(solution)/shard_map/ppermute | solution.py:19
  33.3 7.3 %collective-permute-start.9 = (bf16[288,128]{1,0:T(8,128)(2,1)S(1)}, bf16[288,128]{1,0:T(8,128)(2,1)S(1)}, u32[]{:S(2)}, u32[]{:S(2)}) collective-permute-start(bf16[288,128]{1,0:T(8,128)(2,1)S(1)} %get-tuple-element.34), channel_id=1, source_target_pairs={{0,1},{1,0},{2,3},{3,2},{4,5},{5,4},{6,7},{7,6},{8,9},{9,8},{10,11... | collective-permute-start | bytes 221192 | tf_op jit(solution)/shard_map/ppermute | solution.py:19
  33.4 9.3 %collective-permute-start.10 = (bf16[288,128]{1,0:T(8,128)(2,1)S(1)}, bf16[288,128]{1,0:T(8,128)(2,1)S(1)}, u32[]{:S(2)}, u32[]{:S(2)}) collective-permute-start(bf16[288,128]{1,0:T(8,128)(2,1)S(1)} %get-tuple-element.35), channel_id=1, source_target_pairs={{0,2},{1,3},{2,0},{3,1},{4,6},{5,7},{6,4},{7,5},{8,10},{9,11},{10,... | collective-permute-start | bytes 221192 | tf_op jit(solution)/shard_map/ppermute | solution.py:19
  36.5 8.8 %collective-permute-start.11 = (bf16[288,128]{1,0:T(8,128)(2,1)S(1)}, bf16[288,128]{1,0:T(8,128)(2,1)S(1)}, u32[]{:S(2)}, u32[]{:S(2)}) collective-permute-start(bf16[288,128]{1,0:T(8,128)(2,1)S(1)} %get-tuple-element.36), channel_id=1, source_target_pairs={{0,3},{1,2},{2,1},{3,0},{4,7},{5,6},{6,5},{7,4},{8,11},{9,10},{10,... | collective-permute-start | bytes 221192 | tf_op jit(solution)/shard_map/ppermute | solution.py:19
  37.6 10.7 %collective-permute-start.12 = (bf16[288,128]{1,0:T(8,128)(2,1)S(1)}, bf16[288,128]{1,0:T(8,128)(2,1)S(1)}, u32[]{:S(2)}, u32[]{:S(2)}) collective-permute-start(bf16[288,128]{1,0:T(8,128)(2,1)S(1)} %get-tuple-element.37), channel_id=1, source_target_pairs={{0,4},{1,5},{2,6},{3,7},{4,0},{5,1},{6,2},{7,3},{8,12},{9,13},{10,... | collective-permute-start | bytes 221192 | tf_op jit(solution)/shard_map/ppermute | solution.py:19
  40.3 10.4 %collective-permute-start.13 = (bf16[288,128]{1,0:T(8,128)(2,1)S(1)}, bf16[288,128]{1,0:T(8,128)(2,1)S(1)}, u32[]{:S(2)}, u32[]{:S(2)}) collective-permute-start(bf16[288,128]{1,0:T(8,128)(2,1)S(1)} %get-tuple-element.38), channel_id=1, source_target_pairs={{0,5},{1,4},{2,7},{3,6},{4,1},{5,0},{6,3},{7,2},{8,13},{9,12},{10,... | collective-permute-start | bytes 221192 | tf_op jit(solution)/shard_map/ppermute | solution.py:19
  40.6 10.1 %collective-permute-start.14 = (bf16[288,128]{1,0:T(8,128)(2,1)S(1)}, bf16[288,128]{1,0:T(8,128)(2,1)S(1)}, u32[]{:S(2)}, u32[]{:S(2)}) collective-permute-start(bf16[288,128]{1,0:T(8,128)(2,1)S(1)} %get-tuple-element.39), channel_id=1, source_target_pairs={{0,6},{1,7},{2,4},{3,5},{4,2},{5,3},{6,0},{7,1},{8,14},{9,15},{10,... | collective-permute-start | bytes 221192 | tf_op jit(solution)/shard_map/ppermute | solution.py:19
  42.7 8.0 %collective-permute-start.15 = (bf16[288,128]{1,0:T(8,128)(2,1)S(1)}, bf16[288,128]{1,0:T(8,128)(2,1)S(1)}, u32[]{:S(2)}, u32[]{:S(2)}) collective-permute-start(bf16[288,128]{1,0:T(8,128)(2,1)S(1)} %get-tuple-element.40), channel_id=1, source_target_pairs={{0,7},{1,6},{2,5},{3,4},{4,3},{5,2},{6,1},{7,0},{8,15},{9,14},{10,... | collective-permute-start | bytes 221192 | tf_op jit(solution)/shard_map/ppermute | solution.py:19
  51.3 3.4 %collective-permute-start.16 = (bf16[2,6,32,128]{3,2,1,0:T(8,128)(2,1)S(1)}, bf16[2,6,32,128]{3,2,1,0:T(8,128)(2,1)S(1)}, u32[]{:S(2)}, u32[]{:S(2)}) collective-permute-start(bf16[2,6,32,128]{3,2,1,0:T(8,128)(2,1)S(1)} %get-tuple-element.44), channel_id=1, source_target_pairs={{0,8},{8,0},{16,24},{24,16},{1,9},{9,1},{17,25},{25,17},{2,10},{10... | collective-permute-start | bytes 294920 | tf_op jit(solution)/shard_map/ppermute | solution.py:19
  51.4 5.7 %collective-permute-start.17 = (bf16[2,6,32,128]{3,2,1,0:T(8,128)(2,1)S(1)}, bf16[2,6,32,128]{3,2,1,0:T(8,128)(2,1)S(1)}, u32[]{:S(2)}, u32[]{:S(2)}) collective-permute-start(bf16[2,6,32,128]{3,2,1,0:T(8,128)(2,1)S(1)} %get-tuple-element.45), channel_id=1, source_target_pairs={{0,16},{8,24},{16,0},{24,8},{1,17},{9,25},{17,1},{25,9},{2,18},{10... | collective-permute-start | bytes 294920 | tf_op jit(solution)/shard_map/ppermute | solution.py:19
  51.8 6.5 %collective-permute-start.18 = (bf16[2,6,32,128]{3,2,1,0:T(8,128)(2,1)S(1)}, bf16[2,6,32,128]{3,2,1,0:T(8,128)(2,1)S(1)}, u32[]{:S(2)}, u32[]{:S(2)}) collective-permute-start(bf16[2,6,32,128]{3,2,1,0:T(8,128)(2,1)S(1)} %get-tuple-element.46), channel_id=1, source_target_pairs={{0,24},{8,16},{16,8},{24,0},{1,25},{9,17},{17,9},{25,1},{2,26},{10... | collective-permute-start | bytes 294920 | tf_op jit(solution)/shard_map/ppermute | solution.py:19
where the time goes:
time: 59.7 us; the launch traced here: 59 us
  starting transfers between devices  28.9 us (48%)
  waiting for transfers between devices  16.9 us (28%)
  Pallas kernels  9.77 us (16%)
  between operations  1.51 us (3%)
  local copies, waits for them, and re-layouts  1 us (2%)
  other arithmetic  0.88 us (1%)
    ppermute x17, starting transfers between devices, all_swapped(): lax.ppermute(parts[k], axis, [(i, i ^ k) for i in range(n)])  25.8 us
    ppermute x17, waiting for transfers between devices, all_swapped(): lax.ppermute(parts[k], axis, [(i, i ^ k) for i in range(n)])  16.8 us
    pallas_call x1, Pallas kernels, edge_proj(): pl.pallas_call(edge_proj_kernel, out_shape=jax.ShapeDtypeStruct((2 * slot...  6.04 us
    ppermute x1, starting transfers between devices, per_device(): left_corner = lax.ppermute(corner, 'site', onward)  2.63 us
    pallas_call x1, Pallas kernels, routed_by_tiles(): small_call(bind(join_kernel, n), pieces, ins, [], 'join')(here, *parts)  1.42 us
  transfers between devices with their start and end apart: 19, of which 6 were waited for; matrix products, arithmetic and copies ran while one was open for 0% of the time, Pallas kernels for 13%

commit v1 on v0

--- a/solution.py
+++ b/solution.py
@@ -14,10 +14,14 @@
 HBM = pl.BlockSpec(memory_space=pltpu.HBM)
 
 
-def all_swapped(parts, axis):
+def far_first(n):
+    far, near = range(n // 2, n), range(n // 2 - 1, 0, -1)
+    return (0, *sorted(far, key=lambda k: (k & 1, -k)), *near)
+
+
+def all_swapped(parts, steps, axis):
     n = len(parts)
-    out = {k: lax.ppermute(parts[k], axis, [(i, i ^ k) for i in range(n)]) for k in range(n - 1, 0, -1)}
-    return [parts[0]] + [out[k] for k in range(1, n)]
+    return [lax.ppermute(part, axis, [(i, i ^ k) for i in range(n)]) if k else part for part, k in zip(parts, steps)]
 
 
 def edge_proj_kernel(edge, bedge, proj, wv_ref, edge_buf, bedge_buf, proj_buf, sems):
@@ -84,7 +88,8 @@
     return ground, re.astype(jnp.bfloat16), im.astype(jnp.bfloat16)
 
 
-def spread_kernel(n, here, turn, corner, bcorner, wv, *refs):
+def spread_kernel(steps, here, turn, corner, bcorner, wv, *refs):
+    n = len(steps)
     out, stage = refs[:n], refs[n]
     slots, m = corner.shape[1], corner.shape[2]
     rows = m // n
@@ -96,58 +101,61 @@
         for kind in range(3):
             stage[3 * i + kind] = blocks[kind]
     peak = jnp.full((TILE, m), jnp.max(top), jnp.float32).astype(jnp.bfloat16)
-    for k in range(n):
+    for p, k in enumerate(steps):
         first = pl.multiple_of(jnp.bitwise_xor(here[0], k) * rows, rows)
         for b in range(3 * slots):
-            out[k][b * rows : (b + 1) * rows] = stage[b, pl.ds(first, rows)]
-        out[k][3 * slots * rows :] = peak
-
-
-def route_kernel(n, slots, here, joining, *refs):
+            out[p][b * rows : (b + 1) * rows] = stage[b, pl.ds(first, rows)]
+        out[p][3 * slots * rows :] = peak
+
+
+def route_kernel(steps, slots, here, joining, *refs):
+    n = len(steps)
     pieces, out, held = refs[:n], refs[n : 2 * n], refs[2 * n]
     size = held.shape[1]
-    for k in range(n):
+    for p, k in enumerate(steps):
         d = jnp.bitwise_xor(here[0], k)
         for i in range(slots):
-            held[d * slots + i] = pieces[k][i * size : (i + 1) * size]
+            held[d * slots + i] = pieces[p][i * size : (i + 1) * size]
     top = functools.reduce(jnp.maximum, [piece[slots * size :].astype(jnp.float32) for piece in pieces])
     divisor = jnp.concatenate([top] * (size // TILE), axis=0) + epsilon
-    for k in range(n):
+    for p, k in enumerate(steps):
         t = jnp.bitwise_xor(here[0], k)
         for i in range(slots):
             q = joining[0, t * slots + i]
-            out[k][i * size : (i + 1) * size] = (held[q].astype(jnp.float32) / divisor).astype(jnp.bfloat16)
-
-
-def share_kernel(n, sites, here, *refs):
+            out[p][i * size : (i + 1) * size] = (held[q].astype(jnp.float32) / divisor).astype(jnp.bfloat16)
+
+
+def share_kernel(steps, site_steps, here, *refs):
+    n, sites = len(steps), len(site_steps)
     pieces, shares, stage = refs[:n], refs[n : n + sites], refs[n + sites]
     _, slots, wide, m = shares[0].shape
     rows = m // n
-    for k in range(n):
+    for p, k in enumerate(steps):
         first = pl.multiple_of(jnp.bitwise_xor(here[0], k) * rows, rows)
         for i in range(slots):
             for c in range(2):
                 at = (3 * i + 1 + c) * rows
-                stage[c, i, pl.ds(first, rows)] = pieces[k][at : at + rows]
-    for k in range(sites):
+                stage[c, i, pl.ds(first, rows)] = pieces[p][at : at + rows]
+    for p, k in enumerate(site_steps):
         first = pl.multiple_of(jnp.bitwise_xor(here[1], k) * wide, wide)
         for i in range(slots):
             for c in range(2):
-                shares[k][c, i] = stage[c, i, pl.ds(first, wide)]
-
-
-def join_kernel(n, here, *refs):
+                shares[p][c, i] = stage[c, i, pl.ds(first, wide)]
+
+
+def join_kernel(steps, here, *refs):
+    n = len(steps)
     pieces, new_corner, new_b = refs[:n], refs[n], refs[n + 1]
     _, slots, m, _ = new_corner.shape
     rows = m // n
-    for k in range(n):
+    for p, k in enumerate(steps):
         first = pl.multiple_of(jnp.bitwise_xor(here[0], k) * rows, rows)
         for i in range(slots):
             at = 3 * i * rows
-            new_corner[0, i, pl.ds(first, rows)] = pieces[k][at : at + rows]
+            new_corner[0, i, pl.ds(first, rows)] = pieces[p][at : at + rows]
             for c in range(2):
                 at = (3 * i + 1 + c) * rows
-                new_b[c, 0, i, pl.ds(first, rows)] = pieces[k][at : at + rows]
+                new_b[c, 0, i, pl.ds(first, rows)] = pieces[p][at : at + rows]
 
 
 def routed_by_tiles(turn, corner, bcorner, wv, joining, n, sites):
@@ -156,25 +164,26 @@
     shape = lambda *dims: jax.ShapeDtypeStruct(dims, jnp.bfloat16)
     scratch = lambda *dims: [pltpu.VMEM(dims, jnp.bfloat16)]
     bind = functools.partial
+    steps, site_steps = far_first(n), far_first(sites)
     here = jnp.stack([lax.axis_index("blk"), lax.axis_index("site")]).astype(jnp.int32)
     pieces = [shape(3 * slots * rows + TILE, m)] * n
     kept = scratch(3 * slots, m, m)
-    parts = small_call(bind(spread_kernel, n), pieces, [SMEM] * 2 + [VMEM] * 3, kept, "spread")(
+    parts = small_call(bind(spread_kernel, steps), pieces, [SMEM] * 2 + [VMEM] * 3, kept, "spread")(
         here, turn, corner, bcorner, wv
     )
-    parts = all_swapped(parts, "blk")
+    parts = all_swapped(parts, steps, "blk")
     pieces = [shape(3 * slots * rows, m)] * n
     kept = scratch(n * slots, 3 * rows, m)
-    parts = small_call(bind(route_kernel, n, slots), pieces, [SMEM] * 2 + [VMEM] * n, kept, "route")(
+    parts = small_call(bind(route_kernel, steps, slots), pieces, [SMEM] * 2 + [VMEM] * n, kept, "route")(
         here, joining, *parts
     )
-    parts = all_swapped(parts, "blk")
+    parts = all_swapped(parts, steps, "blk")
     ins = [SMEM] + [VMEM] * n
     pieces = [shape(2, slots, m // sites, m)] * sites
-    shares = small_call(bind(share_kernel, n, sites), pieces, ins, scratch(2, slots, m, m), "share")(here, *parts)
-    shares = all_swapped(shares, "site")
+    shares = small_call(bind(share_kernel, steps, site_steps), pieces, ins, scratch(2, slots, m, m), "share")(here, *parts)
+    shares = all_swapped(shares, site_steps, "site")
     pieces = [shape(1, slots, m, m), shape(2, 1, slots, m, m)]
-    new_corner, new_b = small_call(bind(join_kernel, n), pieces, ins, [], "join")(here, *parts)
+    new_corner, new_b = small_call(bind(join_kernel, steps), pieces, ins, [], "join")(here, *parts)
     return new_corner, new_b, shares
 
 

time: 59.7 us -> 57.2 us (0.958)
  waiting for transfers between devices: 16.9 us -> 11.6 us
  starting transfers between devices: 28.9 us -> 31.9 us
    ppermute x17, waiting for transfers between devices: 16.8 us -> 11.5 us  [all_swapped(): lax.ppermute(part, axis, [(i, i ^ k) for i in range(n)])]
    ppermute x17, starting transfers between devices: 25.8 us -> 28.7 us  [all_swapped(): lax.ppermute(part, axis, [(i, i ^ k) for i in range(n)])]
  transfers between devices with their start and end apart: 19 -> 19, of which waited for: 6 -> 8; matrix products, arithmetic and copies ran while one was open for 0% -> 0% of each run, Pallas kernels for 13% -> 13%
where the time goes in v1:
time: 57.2 us; the launch traced here: 56.6 us
  starting transfers between devices  31.9 us (56%)
  waiting for transfers between devices  11.6 us (20%)
  Pallas kernels  9.76 us (17%)
  between operations  1.5 us (3%)
  local copies, waits for them, and re-layouts  1 us (2%)
  other arithmetic  0.88 us (2%)
    ppermute x17, starting transfers between devices, all_swapped(): lax.ppermute(part, axis, [(i, i ^ k) for i in range(n)])  28.7 us
    ppermute x17, waiting for transfers between devices, all_swapped(): lax.ppermute(part, axis, [(i, i ^ k) for i in range(n)])  11.5 us
    pallas_call x1, Pallas kernels, edge_proj(): pl.pallas_call(edge_proj_kernel, out_shape=jax.ShapeDtypeStruct((2 * slot...  6.04 us
    ppermute x1, starting transfers between devices, per_device(): left_corner = lax.ppermute(corner, 'site', onward)  2.63 us
    pallas_call x1, Pallas kernels, routed_by_tiles(): small_call(bind(join_kernel, steps), pieces, ins, [], 'join')(here, *parts)  1.42 us
  transfers between devices with their start and end apart: 19, of which 8 were waited for; matrix products, arithmetic and copies ran while one was open for 0% of the time, Pallas kernels for 13%

profile of v1, /device:TPU:0, one launch (start us, length us, event | category | flops | bytes accessed | tf_op | source)
XLA Modules:
  0.0 56.6 jit_solution(12064856835930473836)
XLA Ops:
  0.6 0.5 collective-permute-start.1
  1.1 2.6 %collective-permute-start = (bf16[1,6,128,128]{3,2,1,0:T(8,128)(2,1)}, bf16[1,6,128,128]{3,2,1,0:T(8,128)(2,1)S(1)}, u32[]{:S(2)}, u32[]{:S(2)}) collective-permute-start(bf16[1,6,128,128]{3,2,1,0:T(8,128)(2,1)} %param.7), channel_id=1, source_target_pairs={{0,8},{8,16},{16,24},{24,0},{1,9},{9,17},{17,25},{25,1},{2,10},{10... | collective-permute-start | bytes 589832 | tf_op jit(solution)/shard_map/ppermute | solution.py:218
  4.6 0.1 pad_add_fusion.here
  4.6 6.0 %edge_proj.1.wv = bf16[12,128,128]{2,1,0:T(8,128)(2,1)} custom-call(bf16[1,6,128,2304]{3,2,1,0:T(8,128)(2,1)} %edge.1, bf16[1,6,128,2304]{3,2,1,0:T(8,128)(2,1)} %bedge.1, bf16[1,6,2304,128]{3,2,1,0:T(8,128)(2,1)} %proj.1), custom_call_target="tpu_custom_call" | custom-call | flops 905969664 | bytes 10616832 | tf_op jit(solution)/shard_map/edge_proj/pallas_call | solution.py:48
  10.7 0.1 pad_maximum_fusion.turn
  10.8 0.1 collective-permute-done.corner
  10.9 0.0 collective-permute-done.1.bcorner
  10.9 1.0 %copy-done = bf16[12,128,128]{2,1,0:T(8,128)(2,1)S(1)} copy-done((bf16[12,128,128]{2,1,0:T(8,128)(2,1)S(1)}, bf16[12,128,128]{2,1,0:T(8,128)(2,1)}, u32[]{:S(2)}) %copy-start) | copy-done | bytes 393240
  11.9 1.0 %spread.1 = (bf16[304,128]{1,0:T(8,128)(2,1)S(1)}, bf16[304,128]{1,0:T(8,128)(2,1)S(1)}, bf16[304,128]{1,0:T(8,128)(2,1)S(1)}, bf16[304,128]{1,0:T(8,128)(2,1)S(...) custom-call(s32[2]{0:T(128)S(1)} %pad_add_fusion.here, ...), custom_call_target="tpu_custom_call" | custom-call | flops 268435456 | bytes 1048576 | tf_op jit(solution)/shard_map/spread/pallas_call | solution.py:171
  12.9 4.4 %collective-permute-start.2 = (bf16[304,128]{1,0:T(8,128)(2,1)S(1)}, bf16[304,128]{1,0:T(8,128)(2,1)S(1)}, u32[]{:S(2)}, u32[]{:S(2)}) collective-permute-start(bf16[304,128]{1,0:T(8,128)(2,1)S(1)} %get-tuple-element.26), channel_id=1, source_target_pairs={{0,6},{1,7},{2,4},{3,5},{4,2},{5,3},{6,0},{7,1},{8,14},{9,15},{10,... | collective-permute-start | bytes 233480 | tf_op jit(solution)/shard_map/ppermute | solution.py:24
  17.3 0.0 collective-permute-start.3
  17.3 2.8 %collective-permute-start.4 = (bf16[304,128]{1,0:T(8,128)(2,1)S(1)}, bf16[304,128]{1,0:T(8,128)(2,1)S(1)}, u32[]{:S(2)}, u32[]{:S(2)}) collective-permute-start(bf16[304,128]{1,0:T(8,128)(2,1)S(1)} %get-tuple-element.28), channel_id=1, source_target_pairs={{0,7},{1,6},{2,5},{3,4},{4,3},{5,2},{6,1},{7,0},{8,15},{9,14},{10,... | collective-permute-start | bytes 233480 | tf_op jit(solution)/shard_map/ppermute | solution.py:24
  20.2 1.0 %collective-permute-start.5 = (bf16[304,128]{1,0:T(8,128)(2,1)S(1)}, bf16[304,128]{1,0:T(8,128)(2,1)S(1)}, u32[]{:S(2)}, u32[]{:S(2)}) collective-permute-start(bf16[304,128]{1,0:T(8,128)(2,1)S(1)} %get-tuple-element.29), channel_id=1, source_target_pairs={{0,5},{1,4},{2,7},{3,6},{4,1},{5,0},{6,3},{7,2},{8,13},{9,12},{10,... | collective-permute-start | bytes 233480 | tf_op jit(solution)/shard_map/ppermute | solution.py:24
  21.2 2.4 %collective-permute-start.6 = (bf16[304,128]{1,0:T(8,128)(2,1)S(1)}, bf16[304,128]{1,0:T(8,128)(2,1)S(1)}, u32[]{:S(2)}, u32[]{:S(2)}) collective-permute-start(bf16[304,128]{1,0:T(8,128)(2,1)S(1)} %get-tuple-element.30), channel_id=1, source_target_pairs={{0,3},{1,2},{2,1},{3,0},{4,7},{5,6},{6,5},{7,4},{8,11},{9,10},{10,... | collective-permute-start | bytes 233480 | tf_op jit(solution)/shard_map/ppermute | solution.py:24
  23.6 0.0 collective-permute-done.2.refs_1_
  23.6 2.3 %collective-permute-start.7 = (bf16[304,128]{1,0:T(8,128)(2,1)S(1)}, bf16[304,128]{1,0:T(8,128)(2,1)S(1)}, u32[]{:S(2)}, u32[]{:S(2)}) collective-permute-start(bf16[304,128]{1,0:T(8,128)(2,1)S(1)} %get-tuple-element.31), channel_id=1, source_target_pairs={{0,2},{1,3},{2,0},{3,1},{4,6},{5,7},{6,4},{7,5},{8,10},{9,11},{10,... | collective-permute-start | bytes 233480 | tf_op jit(solution)/shard_map/ppermute | solution.py:24
  25.9 0.4 collective-permute-done.3.refs_2_
  26.3 1.5 %collective-permute-start.8 = (bf16[304,128]{1,0:T(8,128)(2,1)S(1)}, bf16[304,128]{1,0:T(8,128)(2,1)S(1)}, u32[]{:S(2)}, u32[]{:S(2)}) collective-permute-start(bf16[304,128]{1,0:T(8,128)(2,1)S(1)} %get-tuple-element.32), channel_id=1, source_target_pairs={{0,1},{1,0},{2,3},{3,2},{4,5},{5,4},{6,7},{7,6},{8,9},{9,8},{10,11... | collective-permute-start | bytes 233480 | tf_op jit(solution)/shard_map/ppermute | solution.py:24
  27.8 0.0 collective-permute-done.4.refs_3_
  27.8 3.3 %collective-permute-done.5.refs_4_ = bf16[304,128]{1,0:T(8,128)(2,1)S(1)} collective-permute-done((bf16[304,128]{1,0:T(8,128)(2,1)S(1)}, bf16[304,128]{1,0:T(8,128)(2,1)S(1)}, u32[]{:S(2)}, u32[]{:S(2)}) %collective-permute-start.5) | collective-permute-done | bytes 77856 | tf_op jit(solution)/shard_map/ppermute | solution.py:24
  31.1 0.0 collective-permute-done.6.refs_5_
  31.1 0.0 collective-permute-done.7.refs_6_
  31.1 0.7 %collective-permute-done.8.refs_7_ = bf16[304,128]{1,0:T(8,128)(2,1)S(1)} collective-permute-done((bf16[304,128]{1,0:T(8,128)(2,1)S(1)}, bf16[304,128]{1,0:T(8,128)(2,1)S(1)}, u32[]{:S(2)}, u32[]{:S(2)}) %collective-permute-start.8) | collective-permute-done | bytes 77856 | tf_op jit(solution)/shard_map/ppermute | solution.py:24
  31.9 0.0 copy-done.1
  31.9 0.7 %route.1 = (bf16[288,128]{1,0:T(8,128)(2,1)S(1)}, bf16[288,128]{1,0:T(8,128)(2,1)S(1)}, bf16[288,128]{1,0:T(8,128)(2,1)S(1)}, bf16[288,128]{1,0:T(8,128)(2,1)S(1...) custom-call(s32[2]{0:T(128)S(1)} %pad_add_fusion.here, ...), custom_call_target="tpu_custom_call" | custom-call | flops 268435456 | bytes 1048576 | tf_op jit(solution)/shard_map/route/pallas_call | solution.py:177
  32.6 3.4 %collective-permute-start.9 = (bf16[288,128]{1,0:T(8,128)(2,1)S(1)}, bf16[288,128]{1,0:T(8,128)(2,1)S(1)}, u32[]{:S(2)}, u32[]{:S(2)}) collective-permute-start(bf16[288,128]{1,0:T(8,128)(2,1)S(1)} %get-tuple-element.34), channel_id=1, source_target_pairs={{0,6},{1,7},{2,4},{3,5},{4,2},{5,3},{6,0},{7,1},{8,14},{9,15},{10,... | collective-permute-start | bytes 221192 | tf_op jit(solution)/shard_map/ppermute | solution.py:24
  36.0 0.0 collective-permute-start.10
  36.0 1.2 %collective-permute-start.11 = (bf16[288,128]{1,0:T(8,128)(2,1)S(1)}, bf16[288,128]{1,0:T(8,128)(2,1)S(1)}, u32[]{:S(2)}, u32[]{:S(2)}) collective-permute-start(bf16[288,128]{1,0:T(8,128)(2,1)S(1)} %get-tuple-element.36), channel_id=1, source_target_pairs={{0,7},{1,6},{2,5},{3,4},{4,3},{5,2},{6,1},{7,0},{8,15},{9,14},{10,... | collective-permute-start | bytes 221192 | tf_op jit(solution)/shard_map/ppermute | solution.py:24
  37.2 2.6 %collective-permute-start.12 = (bf16[288,128]{1,0:T(8,128)(2,1)S(1)}, bf16[288,128]{1,0:T(8,128)(2,1)S(1)}, u32[]{:S(2)}, u32[]{:S(2)}) collective-permute-start(bf16[288,128]{1,0:T(8,128)(2,1)S(1)} %get-tuple-element.37), channel_id=1, source_target_pairs={{0,5},{1,4},{2,7},{3,6},{4,1},{5,0},{6,3},{7,2},{8,13},{9,12},{10,... | collective-permute-start | bytes 221192 | tf_op jit(solution)/shard_map/ppermute | solution.py:24
  39.8 2.4 %collective-permute-start.13 = (bf16[288,128]{1,0:T(8,128)(2,1)S(1)}, bf16[288,128]{1,0:T(8,128)(2,1)S(1)}, u32[]{:S(2)}, u32[]{:S(2)}) collective-permute-start(bf16[288,128]{1,0:T(8,128)(2,1)S(1)} %get-tuple-element.38), channel_id=1, source_target_pairs={{0,3},{1,2},{2,1},{3,0},{4,7},{5,6},{6,5},{7,4},{8,11},{9,10},{10,... | collective-permute-start | bytes 221192 | tf_op jit(solution)/shard_map/ppermute | solution.py:24
  42.1 0.0 collective-permute-done.9.refs_1_
  42.1 1.1 %collective-permute-start.14 = (bf16[288,128]{1,0:T(8,128)(2,1)S(1)}, bf16[288,128]{1,0:T(8,128)(2,1)S(1)}, u32[]{:S(2)}, u32[]{:S(2)}) collective-permute-start(bf16[288,128]{1,0:T(8,128)(2,1)S(1)} %get-tuple-element.39), channel_id=1, source_target_pairs={{0,2},{1,3},{2,0},{3,1},{4,6},{5,7},{6,4},{7,5},{8,10},{9,11},{10,... | collective-permute-start | bytes 221192 | tf_op jit(solution)/shard_map/ppermute | solution.py:24
  43.2 2.5 %collective-permute-done.10.refs_2_ = bf16[288,128]{1,0:T(8,128)(2,1)S(1)} collective-permute-done((bf16[288,128]{1,0:T(8,128)(2,1)S(1)}, bf16[288,128]{1,0:T(8,128)(2,1)S(1)}, u32[]{:S(2)}, u32[]{:S(2)}) %collective-permute-start.10) | collective-permute-done | bytes 73760 | tf_op jit(solution)/shard_map/ppermute | solution.py:24
  45.7 1.4 %collective-permute-start.15 = (bf16[288,128]{1,0:T(8,128)(2,1)S(1)}, bf16[288,128]{1,0:T(8,128)(2,1)S(1)}, u32[]{:S(2)}, u32[]{:S(2)}) collective-permute-start(bf16[288,128]{1,0:T(8,128)(2,1)S(1)} %get-tuple-element.40), channel_id=1, source_target_pairs={{0,1},{1,0},{2,3},{3,2},{4,5},{5,4},{6,7},{7,6},{8,9},{9,8},{10,11... | collective-permute-start | bytes 221192 | tf_op jit(solution)/shard_map/ppermute | solution.py:24
  47.1 0.0 collective-permute-done.11.refs_3_
  47.1 1.5 %collective-permute-done.12.refs_4_ = bf16[288,128]{1,0:T(8,128)(2,1)S(1)} collective-permute-done((bf16[288,128]{1,0:T(8,128)(2,1)S(1)}, bf16[288,128]{1,0:T(8,128)(2,1)S(1)}, u32[]{:S(2)}, u32[]{:S(2)}) %collective-permute-start.12) | collective-permute-done | bytes 73760 | tf_op jit(solution)/shard_map/ppermute | solution.py:24
  48.6 0.0 collective-permute-done.13.refs_5_
  48.6 0.0 collective-permute-done.14.refs_6_
  48.6 1.5 %collective-permute-done.15.refs_7_ = bf16[288,128]{1,0:T(8,128)(2,1)S(1)} collective-permute-done((bf16[288,128]{1,0:T(8,128)(2,1)S(1)}, bf16[288,128]{1,0:T(8,128)(2,1)S(1)}, u32[]{:S(2)}, u32[]{:S(2)}) %collective-permute-start.15) | collective-permute-done | bytes 73760 | tf_op jit(solution)/shard_map/ppermute | solution.py:24
  50.0 0.6 %share.1 = (bf16[2,6,32,128]{3,2,1,0:T(8,128)(2,1)S(1)}, bf16[2,6,32,128]{3,2,1,0:T(8,128)(2,1)S(1)}, bf16[2,6,32,128]{3,2,1,0:T(8,128)(2,1)S(1)}, bf16[2,6,32,128]{3,2,1,0:T(8,128)(2,1)S(1)}) custom-call(s32[2]{0:T(128)S(1)} %pad_add_fusion.here, bf16[288,128]{1,0:T(8,128)(2,1)S(1)} %get-tuple-element.33.refs_0_, ...), custom_call_target="tpu_custom_call" | custom-call | flops 268435456 | bytes 1048576 | tf_op jit(solution)/shard_map/share/pallas_call | solution.py:183
  50.6 0.1 collective-permute-start.16
  50.8 0.0 collective-permute-start.17
  50.8 2.0 %collective-permute-start.18 = (bf16[2,6,32,128]{3,2,1,0:T(8,128)(2,1)S(1)}, bf16[2,6,32,128]{3,2,1,0:T(8,128)(2,1)S(1)}, u32[]{:S(2)}, u32[]{:S(2)}) collective-permute-start(bf16[2,6,32,128]{3,2,1,0:T(8,128)(2,1)S(1)} %get-tuple-element.46), channel_id=1, source_target_pairs={{0,8},{8,0},{16,24},{24,16},{1,9},{9,1},{17,25},{25,17},{2,10},{10... | collective-permute-start | bytes 294920 | tf_op jit(solution)/shard_map/ppermute | solution.py:24
  52.9 1.4 %join.1 = (bf16[1,6,128,128]{3,2,1,0:T(8,128)(2,1)}, bf16[2,1,6,128,128]{4,3,2,1,0:T(8,128)(2,1)}) custom-call(s32[2]{0:T(128)S(1)} %pad_add_fusion.here, bf16[288,128]{1,0:T(8,128)(2,1)S(1)} %get-tuple-element.33.refs_0_, bf16[288,128]{1,0:T(8,128)(2,1)S(1)} %collective-permute-done.9.refs_1_, bf16[288,128]{1,0:T(8,128)(2,1)S(1)} %collective-permute-done.10.refs_2_, ...), custom_call_target="tpu_custom_call" | custom-call | flops 268435456 | bytes 1048576 | tf_op jit(solution)/shard_map/join/pallas_call | solution.py:186
  54.3 1.6 %collective-permute-done.16 = bf16[2,6,32,128]{3,2,1,0:T(8,128)(2,1)S(1)} collective-permute-done((bf16[2,6,32,128]{3,2,1,0:T(8,128)(2,1)S(1)}, bf16[2,6,32,128]{3,2,1,0:T(8,128)(2,1)S(1)}, u32[]{:S(2)}, u32[]{:S(2)}) %collective-permute-start.16) | collective-permute-done | bytes 98336 | tf_op jit(solution)/shard_map/ppermute | solution.py:24
  55.9 0.0 collective-permute-done.17
  55.9 0.0 collective-permute-done.18
  55.9 0.7 %convert_add_fusion = f32[2,6,32,128]{3,2,1,0:T(8,128)} fusion(bf16[2,6,32,128]{3,2,1,0:T(8,128)(2,1)S(1)} %collective-permute-done.18, bf16[2,6,32,128]{3,2,1,0:T(8,128)(2,1)S(1)} %collective-permute-done.17, bf16[2,6,32,128]{3,2,1,0:T(8,128)(2,1)S(1)} %collective-permute-done.16, bf16[2,6,32,128]{3,2,1,0:T(8,128)(2,1)S(1)} %get-tuple-element.43), kind=kLoop, calls=%fused_computation | loop fusion | flops 344064 | bytes 589824 | tf_op jit(solution)/shard_map/add | solution.py:225
  (2 shorter events, 0.0 us)
Async XLA Ops:
  0.6 10.2 %collective-permute-start.1 = (bf16[2,1,6,128,128]{4,3,2,1,0:T(8,128)(2,1)}, bf16[2,1,6,128,128]{4,3,2,1,0:T(8,128)(2,1)S(1)}, u32[]{:S(2)}, u32[]{:S(2)}) collective-permute-start(bf16[2,1,6,128,128]{4,3,2,1,0:T(8,128)(2,1)} %param.8), channel_id=1, source_target_pairs={{0,8},{8,16},{16,24},{24,0},{1,9},{9,17},{17,25},{25,1},{2,10},{10... | collective-permute-start | bytes 1179656 | tf_op jit(solution)/shard_map/ppermute | solution.py:219
  1.1 9.7 %collective-permute-start = (bf16[1,6,128,128]{3,2,1,0:T(8,128)(2,1)}, bf16[1,6,128,128]{3,2,1,0:T(8,128)(2,1)S(1)}, u32[]{:S(2)}, u32[]{:S(2)}) collective-permute-start(bf16[1,6,128,128]{3,2,1,0:T(8,128)(2,1)} %param.7), channel_id=1, source_target_pairs={{0,8},{8,16},{16,24},{24,0},{1,9},{9,17},{17,25},{25,1},{2,10},{10... | collective-permute-start | bytes 589832 | tf_op jit(solution)/shard_map/ppermute | solution.py:218
  4.6 27.2 %copy-start.1 = (s32[1,48]{1,0:T(1,128)S(1)}, s32[1,48]{1,0:T(1,128)}, u32[]{:S(2)}) copy-start(s32[1,48]{1,0:T(1,128)} %joining.1) | copy-start | bytes 580
  10.9 1.0 %copy-start = (bf16[12,128,128]{2,1,0:T(8,128)(2,1)S(1)}, bf16[12,128,128]{2,1,0:T(8,128)(2,1)}, u32[]{:S(2)}) copy-start(bf16[12,128,128]{2,1,0:T(8,128)(2,1)} %edge_proj.1.wv) | copy-start | bytes 1179652
  12.9 10.7 %collective-permute-start.2 = (bf16[304,128]{1,0:T(8,128)(2,1)S(1)}, bf16[304,128]{1,0:T(8,128)(2,1)S(1)}, u32[]{:S(2)}, u32[]{:S(2)}) collective-permute-start(bf16[304,128]{1,0:T(8,128)(2,1)S(1)} %get-tuple-element.26), channel_id=1, source_target_pairs={{0,6},{1,7},{2,4},{3,5},{4,2},{5,3},{6,0},{7,1},{8,14},{9,15},{10,... | collective-permute-start | bytes 233480 | tf_op jit(solution)/shard_map/ppermute | solution.py:24
  17.3 9.0 %collective-permute-start.3 = (bf16[304,128]{1,0:T(8,128)(2,1)S(1)}, bf16[304,128]{1,0:T(8,128)(2,1)S(1)}, u32[]{:S(2)}, u32[]{:S(2)}) collective-permute-start(bf16[304,128]{1,0:T(8,128)(2,1)S(1)} %get-tuple-element.27), channel_id=1, source_target_pairs={{0,4},{1,5},{2,6},{3,7},{4,0},{5,1},{6,2},{7,3},{8,12},{9,13},{10,... | collective-permute-start | bytes 233480 | tf_op jit(solution)/shard_map/ppermute | solution.py:24
  17.3 10.5 %collective-permute-start.4 = (bf16[304,128]{1,0:T(8,128)(2,1)S(1)}, bf16[304,128]{1,0:T(8,128)(2,1)S(1)}, u32[]{:S(2)}, u32[]{:S(2)}) collective-permute-start(bf16[304,128]{1,0:T(8,128)(2,1)S(1)} %get-tuple-element.28), channel_id=1, source_target_pairs={{0,7},{1,6},{2,5},{3,4},{4,3},{5,2},{6,1},{7,0},{8,15},{9,14},{10,... | collective-permute-start | bytes 233480 | tf_op jit(solution)/shard_map/ppermute | solution.py:24
  20.2 11.0 %collective-permute-start.5 = (bf16[304,128]{1,0:T(8,128)(2,1)S(1)}, bf16[304,128]{1,0:T(8,128)(2,1)S(1)}, u32[]{:S(2)}, u32[]{:S(2)}) collective-permute-start(bf16[304,128]{1,0:T(8,128)(2,1)S(1)} %get-tuple-element.29), channel_id=1, source_target_pairs={{0,5},{1,4},{2,7},{3,6},{4,1},{5,0},{6,3},{7,2},{8,13},{9,12},{10,... | collective-permute-start | bytes 233480 | tf_op jit(solution)/shard_map/ppermute | solution.py:24
  21.2 9.9 %collective-permute-start.6 = (bf16[304,128]{1,0:T(8,128)(2,1)S(1)}, bf16[304,128]{1,0:T(8,128)(2,1)S(1)}, u32[]{:S(2)}, u32[]{:S(2)}) collective-permute-start(bf16[304,128]{1,0:T(8,128)(2,1)S(1)} %get-tuple-element.30), channel_id=1, source_target_pairs={{0,3},{1,2},{2,1},{3,0},{4,7},{5,6},{6,5},{7,4},{8,11},{9,10},{10,... | collective-permute-start | bytes 233480 | tf_op jit(solution)/shard_map/ppermute | solution.py:24
  23.6 7.6 %collective-permute-start.7 = (bf16[304,128]{1,0:T(8,128)(2,1)S(1)}, bf16[304,128]{1,0:T(8,128)(2,1)S(1)}, u32[]{:S(2)}, u32[]{:S(2)}) collective-permute-start(bf16[304,128]{1,0:T(8,128)(2,1)S(1)} %get-tuple-element.31), channel_id=1, source_target_pairs={{0,2},{1,3},{2,0},{3,1},{4,6},{5,7},{6,4},{7,5},{8,10},{9,11},{10,... | collective-permute-start | bytes 233480 | tf_op jit(solution)/shard_map/ppermute | solution.py:24
  26.3 5.6 %collective-permute-start.8 = (bf16[304,128]{1,0:T(8,128)(2,1)S(1)}, bf16[304,128]{1,0:T(8,128)(2,1)S(1)}, u32[]{:S(2)}, u32[]{:S(2)}) collective-permute-start(bf16[304,128]{1,0:T(8,128)(2,1)S(1)} %get-tuple-element.32), channel_id=1, source_target_pairs={{0,1},{1,0},{2,3},{3,2},{4,5},{5,4},{6,7},{7,6},{8,9},{9,8},{10,11... | collective-permute-start | bytes 233480 | tf_op jit(solution)/shard_map/ppermute | solution.py:24
  32.6 9.6 %collective-permute-start.9 = (bf16[288,128]{1,0:T(8,128)(2,1)S(1)}, bf16[288,128]{1,0:T(8,128)(2,1)S(1)}, u32[]{:S(2)}, u32[]{:S(2)}) collective-permute-start(bf16[288,128]{1,0:T(8,128)(2,1)S(1)} %get-tuple-element.34), channel_id=1, source_target_pairs={{0,6},{1,7},{2,4},{3,5},{4,2},{5,3},{6,0},{7,1},{8,14},{9,15},{10,... | collective-permute-start | bytes 221192 | tf_op jit(solution)/shard_map/ppermute | solution.py:24
  36.0 9.7 %collective-permute-start.10 = (bf16[288,128]{1,0:T(8,128)(2,1)S(1)}, bf16[288,128]{1,0:T(8,128)(2,1)S(1)}, u32[]{:S(2)}, u32[]{:S(2)}) collective-permute-start(bf16[288,128]{1,0:T(8,128)(2,1)S(1)} %get-tuple-element.35), channel_id=1, source_target_pairs={{0,4},{1,5},{2,6},{3,7},{4,0},{5,1},{6,2},{7,3},{8,12},{9,13},{10,... | collective-permute-start | bytes 221192 | tf_op jit(solution)/shard_map/ppermute | solution.py:24
  36.0 11.1 %collective-permute-start.11 = (bf16[288,128]{1,0:T(8,128)(2,1)S(1)}, bf16[288,128]{1,0:T(8,128)(2,1)S(1)}, u32[]{:S(2)}, u32[]{:S(2)}) collective-permute-start(bf16[288,128]{1,0:T(8,128)(2,1)S(1)} %get-tuple-element.36), channel_id=1, source_target_pairs={{0,7},{1,6},{2,5},{3,4},{4,3},{5,2},{6,1},{7,0},{8,15},{9,14},{10,... | collective-permute-start | bytes 221192 | tf_op jit(solution)/shard_map/ppermute | solution.py:24
  37.2 11.4 %collective-permute-start.12 = (bf16[288,128]{1,0:T(8,128)(2,1)S(1)}, bf16[288,128]{1,0:T(8,128)(2,1)S(1)}, u32[]{:S(2)}, u32[]{:S(2)}) collective-permute-start(bf16[288,128]{1,0:T(8,128)(2,1)S(1)} %get-tuple-element.37), channel_id=1, source_target_pairs={{0,5},{1,4},{2,7},{3,6},{4,1},{5,0},{6,3},{7,2},{8,13},{9,12},{10,... | collective-permute-start | bytes 221192 | tf_op jit(solution)/shard_map/ppermute | solution.py:24
  39.8 8.8 %collective-permute-start.13 = (bf16[288,128]{1,0:T(8,128)(2,1)S(1)}, bf16[288,128]{1,0:T(8,128)(2,1)S(1)}, u32[]{:S(2)}, u32[]{:S(2)}) collective-permute-start(bf16[288,128]{1,0:T(8,128)(2,1)S(1)} %get-tuple-element.38), channel_id=1, source_target_pairs={{0,3},{1,2},{2,1},{3,0},{4,7},{5,6},{6,5},{7,4},{8,11},{9,10},{10,... | collective-permute-start | bytes 221192 | tf_op jit(solution)/shard_map/ppermute | solution.py:24
  42.1 6.4 %collective-permute-start.14 = (bf16[288,128]{1,0:T(8,128)(2,1)S(1)}, bf16[288,128]{1,0:T(8,128)(2,1)S(1)}, u32[]{:S(2)}, u32[]{:S(2)}) collective-permute-start(bf16[288,128]{1,0:T(8,128)(2,1)S(1)} %get-tuple-element.39), channel_id=1, source_target_pairs={{0,2},{1,3},{2,0},{3,1},{4,6},{5,7},{6,4},{7,5},{8,10},{9,11},{10,... | collective-permute-start | bytes 221192 | tf_op jit(solution)/shard_map/ppermute | solution.py:24
  45.7 4.4 %collective-permute-start.15 = (bf16[288,128]{1,0:T(8,128)(2,1)S(1)}, bf16[288,128]{1,0:T(8,128)(2,1)S(1)}, u32[]{:S(2)}, u32[]{:S(2)}) collective-permute-start(bf16[288,128]{1,0:T(8,128)(2,1)S(1)} %get-tuple-element.40), channel_id=1, source_target_pairs={{0,1},{1,0},{2,3},{3,2},{4,5},{5,4},{6,7},{7,6},{8,9},{9,8},{10,11... | collective-permute-start | bytes 221192 | tf_op jit(solution)/shard_map/ppermute | solution.py:24
  50.6 5.2 %collective-permute-start.16 = (bf16[2,6,32,128]{3,2,1,0:T(8,128)(2,1)S(1)}, bf16[2,6,32,128]{3,2,1,0:T(8,128)(2,1)S(1)}, u32[]{:S(2)}, u32[]{:S(2)}) collective-permute-start(bf16[2,6,32,128]{3,2,1,0:T(8,128)(2,1)S(1)} %get-tuple-element.44), channel_id=1, source_target_pairs={{0,16},{8,24},{16,0},{24,8},{1,17},{9,25},{17,1},{25,9},{2,18},{10... | collective-permute-start | bytes 294920 | tf_op jit(solution)/shard_map/ppermute | solution.py:24
  50.8 5.1 %collective-permute-start.17 = (bf16[2,6,32,128]{3,2,1,0:T(8,128)(2,1)S(1)}, bf16[2,6,32,128]{3,2,1,0:T(8,128)(2,1)S(1)}, u32[]{:S(2)}, u32[]{:S(2)}) collective-permute-start(bf16[2,6,32,128]{3,2,1,0:T(8,128)(2,1)S(1)} %get-tuple-element.45), channel_id=1, source_target_pairs={{0,24},{8,16},{16,8},{24,0},{1,25},{9,17},{17,9},{25,1},{2,26},{10... | collective-permute-start | bytes 294920 | tf_op jit(solution)/shard_map/ppermute | solution.py:24
  50.8 5.1 %collective-permute-start.18 = (bf16[2,6,32,128]{3,2,1,0:T(8,128)(2,1)S(1)}, bf16[2,6,32,128]{3,2,1,0:T(8,128)(2,1)S(1)}, u32[]{:S(2)}, u32[]{:S(2)}) collective-permute-start(bf16[2,6,32,128]{3,2,1,0:T(8,128)(2,1)S(1)} %get-tuple-element.46), channel_id=1, source_target_pairs={{0,8},{8,0},{16,24},{24,16},{1,9},{9,1},{17,25},{25,17},{2,10},{10... | collective-permute-start | bytes 294920 | tf_op jit(solution)/shard_map/ppermute | solution.py:24

commit v2 on v1

--- a/solution.py
+++ b/solution.py
@@ -9,6 +9,7 @@
 
 epsilon = 1e-06
 TILE = 16
+AHEAD = 2
 VMEM = pl.BlockSpec(memory_space=pltpu.VMEM)
 SMEM = pl.BlockSpec(memory_space=pltpu.SMEM)
 HBM = pl.BlockSpec(memory_space=pltpu.HBM)
@@ -31,11 +32,14 @@
         [pltpu.make_async_copy(src.at[0, i], buf.at[i], sems.at[3 * i + a]) for a, (src, buf) in enumerate(pairs)]
         for i in range(slots)
     ]
-    for group in copies:
+    for group in copies[:AHEAD]:
         for copy in group:
             copy.start()
     dot = functools.partial(jnp.dot, preferred_element_type=jnp.float32)
     for i, (first, second, third) in enumerate(copies):
+        for group in copies[i + AHEAD : i + AHEAD + 1]:
+            for copy in group:
+                copy.start()
         first.wait()
         second.wait()
         wv_ref[2 * i] = dot(edge_buf[i], proj_buf[i]).astype(wv_ref.dtype)
@@ -59,7 +63,7 @@
         cost_estimate=pl.CostEstimate(
             flops=4 * slots * m * k * m, bytes_accessed=6 * slots * m * k, transcendentals=0
         ),
-        compiler_params=pltpu.CompilerParams(vmem_limit_bytes=60 << 20),
+        compiler_params=pltpu.CompilerParams(vmem_limit_bytes=52 << 20),
         name="edge_proj",
     )(edge, bedge, proj)
 

time: 57.2 us -> 56.2 us (0.983)
  local copies, waits for them, and re-layouts: 1 us -> 0.01 us
  Pallas kernels: 9.76 us -> 9.02 us
  waiting for transfers between devices: 11.6 us -> 12.3 us
    unnamed x4 -> x2, local copies, waits for them, and re-layouts: 1 us -> 0.01 us
    ppermute x1, waiting for transfers between devices: 0.1 us -> 0.84 us  [per_device(): left_corner = lax.ppermute(corner, 'site', onward)]
    pallas_call x1, Pallas kernels: 6.04 us -> 5.29 us  [edge_proj(): pl.pallas_call(edge_proj_kernel, out_shape=jax.ShapeDtypeStruct((2 * slot...]
  transfers between devices with their start and end apart: 19 -> 19, of which waited for: 8 -> 8; matrix products, arithmetic and copies ran while one was open for 0% -> 0% of each run, Pallas kernels for 13% -> 12%
where the time goes in v2:
time: 56.2 us; the launch traced here: 55.6 us
  starting transfers between devices  31.9 us (57%)
  waiting for transfers between devices  12.3 us (22%)
  Pallas kernels  9.02 us (16%)
  between operations  1.5 us (3%)
  other arithmetic  0.88 us (2%)
    ppermute x17, starting transfers between devices, all_swapped(): lax.ppermute(part, axis, [(i, i ^ k) for i in range(n)])  28.8 us
    ppermute x17, waiting for transfers between devices, all_swapped(): lax.ppermute(part, axis, [(i, i ^ k) for i in range(n)])  11.5 us
    pallas_call x1, Pallas kernels, edge_proj(): pl.pallas_call(edge_proj_kernel, out_shape=jax.ShapeDtypeStruct((2 * slot...  5.29 us
    ppermute x1, starting transfers between devices, per_device(): left_corner = lax.ppermute(corner, 'site', onward)  2.63 us
    pallas_call x1, Pallas kernels, routed_by_tiles(): small_call(bind(join_kernel, steps), pieces, ins, [], 'join')(here, *parts)  1.42 us
  transfers between devices with their start and end apart: 19, of which 8 were waited for; matrix products, arithmetic and copies ran while one was open for 0% of the time, Pallas kernels for 12%

profile of v2, /device:TPU:0, one launch (start us, length us, event | category | flops | bytes accessed | tf_op | source)
XLA Modules:
  0.0 55.6 jit_solution(9333047812208199932)
XLA Ops:
  0.6 0.5 collective-permute-start.1
  1.1 2.6 %collective-permute-start = (bf16[1,6,128,128]{3,2,1,0:T(8,128)(2,1)}, bf16[1,6,128,128]{3,2,1,0:T(8,128)(2,1)S(1)}, u32[]{:S(2)}, u32[]{:S(2)}) collective-permute-start(bf16[1,6,128,128]{3,2,1,0:T(8,128)(2,1)} %param.7), channel_id=1, source_target_pairs={{0,8},{8,16},{16,24},{24,0},{1,9},{9,17},{17,25},{25,1},{2,10},{10... | collective-permute-start | bytes 589832 | tf_op jit(solution)/shard_map/ppermute | solution.py:222
  4.6 0.1 pad_add_fusion.here
  4.6 0.0 copy-start
  4.6 5.3 %edge_proj.1.wv = bf16[12,128,128]{2,1,0:T(8,128)(2,1)S(1)} custom-call(bf16[1,6,128,2304]{3,2,1,0:T(8,128)(2,1)} %edge.1, bf16[1,6,128,2304]{3,2,1,0:T(8,128)(2,1)} %bedge.1, bf16[1,6,2304,128]{3,2,1,0:T(8,128)(2,1)} %proj.1), custom_call_target="tpu_custom_call" | custom-call | flops 905969664 | bytes 10616832 | tf_op jit(solution)/shard_map/edge_proj/pallas_call | solution.py:52
  9.9 0.1 pad_maximum_fusion.turn
  10.0 0.8 %collective-permute-done.corner = bf16[1,6,128,128]{3,2,1,0:T(8,128)(2,1)S(1)} collective-permute-done((bf16[1,6,128,128]{3,2,1,0:T(8,128)(2,1)}, bf16[1,6,128,128]{3,2,1,0:T(8,128)(2,1)S(1)}, u32[]{:S(2)}, u32[]{:S(2)}) %collective-permute-start) | collective-permute-done | bytes 196640 | tf_op jit(solution)/shard_map/ppermute | solution.py:222
  10.9 0.0 collective-permute-done.1.bcorner
  10.9 1.0 %spread.1 = (bf16[304,128]{1,0:T(8,128)(2,1)S(1)}, bf16[304,128]{1,0:T(8,128)(2,1)S(1)}, bf16[304,128]{1,0:T(8,128)(2,1)S(1)}, bf16[304,128]{1,0:T(8,128)(2,1)S(...) custom-call(s32[2]{0:T(128)S(1)} %pad_add_fusion.here, ...), custom_call_target="tpu_custom_call" | custom-call | flops 268435456 | bytes 1048576 | tf_op jit(solution)/shard_map/spread/pallas_call | solution.py:175
  11.9 4.4 %collective-permute-start.2 = (bf16[304,128]{1,0:T(8,128)(2,1)S(1)}, bf16[304,128]{1,0:T(8,128)(2,1)S(1)}, u32[]{:S(2)}, u32[]{:S(2)}) collective-permute-start(bf16[304,128]{1,0:T(8,128)(2,1)S(1)} %get-tuple-element.26), channel_id=1, source_target_pairs={{0,6},{1,7},{2,4},{3,5},{4,2},{5,3},{6,0},{7,1},{8,14},{9,15},{10,... | collective-permute-start | bytes 233480 | tf_op jit(solution)/shard_map/ppermute | solution.py:25
  16.3 0.0 collective-permute-start.3
  16.3 2.8 %collective-permute-start.4 = (bf16[304,128]{1,0:T(8,128)(2,1)S(1)}, bf16[304,128]{1,0:T(8,128)(2,1)S(1)}, u32[]{:S(2)}, u32[]{:S(2)}) collective-permute-start(bf16[304,128]{1,0:T(8,128)(2,1)S(1)} %get-tuple-element.28), channel_id=1, source_target_pairs={{0,7},{1,6},{2,5},{3,4},{4,3},{5,2},{6,1},{7,0},{8,15},{9,14},{10,... | collective-permute-start | bytes 233480 | tf_op jit(solution)/shard_map/ppermute | solution.py:25
  19.2 1.0 %collective-permute-start.5 = (bf16[304,128]{1,0:T(8,128)(2,1)S(1)}, bf16[304,128]{1,0:T(8,128)(2,1)S(1)}, u32[]{:S(2)}, u32[]{:S(2)}) collective-permute-start(bf16[304,128]{1,0:T(8,128)(2,1)S(1)} %get-tuple-element.29), channel_id=1, source_target_pairs={{0,5},{1,4},{2,7},{3,6},{4,1},{5,0},{6,3},{7,2},{8,13},{9,12},{10,... | collective-permute-start | bytes 233480 | tf_op jit(solution)/shard_map/ppermute | solution.py:25
  20.2 2.4 %collective-permute-start.6 = (bf16[304,128]{1,0:T(8,128)(2,1)S(1)}, bf16[304,128]{1,0:T(8,128)(2,1)S(1)}, u32[]{:S(2)}, u32[]{:S(2)}) collective-permute-start(bf16[304,128]{1,0:T(8,128)(2,1)S(1)} %get-tuple-element.30), channel_id=1, source_target_pairs={{0,3},{1,2},{2,1},{3,0},{4,7},{5,6},{6,5},{7,4},{8,11},{9,10},{10,... | collective-permute-start | bytes 233480 | tf_op jit(solution)/shard_map/ppermute | solution.py:25
  22.6 0.0 collective-permute-done.2.refs_1_
  22.6 2.4 %collective-permute-start.7 = (bf16[304,128]{1,0:T(8,128)(2,1)S(1)}, bf16[304,128]{1,0:T(8,128)(2,1)S(1)}, u32[]{:S(2)}, u32[]{:S(2)}) collective-permute-start(bf16[304,128]{1,0:T(8,128)(2,1)S(1)} %get-tuple-element.31), channel_id=1, source_target_pairs={{0,2},{1,3},{2,0},{3,1},{4,6},{5,7},{6,4},{7,5},{8,10},{9,11},{10,... | collective-permute-start | bytes 233480 | tf_op jit(solution)/shard_map/ppermute | solution.py:25
  24.9 0.3 collective-permute-done.3.refs_2_
  25.3 1.5 %collective-permute-start.8 = (bf16[304,128]{1,0:T(8,128)(2,1)S(1)}, bf16[304,128]{1,0:T(8,128)(2,1)S(1)}, u32[]{:S(2)}, u32[]{:S(2)}) collective-permute-start(bf16[304,128]{1,0:T(8,128)(2,1)S(1)} %get-tuple-element.32), channel_id=1, source_target_pairs={{0,1},{1,0},{2,3},{3,2},{4,5},{5,4},{6,7},{7,6},{8,9},{9,8},{10,11... | collective-permute-start | bytes 233480 | tf_op jit(solution)/shard_map/ppermute | solution.py:25
  26.8 0.0 collective-permute-done.4.refs_3_
  26.8 3.3 %collective-permute-done.5.refs_4_ = bf16[304,128]{1,0:T(8,128)(2,1)S(1)} collective-permute-done((bf16[304,128]{1,0:T(8,128)(2,1)S(1)}, bf16[304,128]{1,0:T(8,128)(2,1)S(1)}, u32[]{:S(2)}, u32[]{:S(2)}) %collective-permute-start.5) | collective-permute-done | bytes 77856 | tf_op jit(solution)/shard_map/ppermute | solution.py:25
  30.1 0.0 collective-permute-done.6.refs_5_
  30.1 0.0 collective-permute-done.7.refs_6_
  30.1 0.7 %collective-permute-done.8.refs_7_ = bf16[304,128]{1,0:T(8,128)(2,1)S(1)} collective-permute-done((bf16[304,128]{1,0:T(8,128)(2,1)S(1)}, bf16[304,128]{1,0:T(8,128)(2,1)S(1)}, u32[]{:S(2)}, u32[]{:S(2)}) %collective-permute-start.8) | collective-permute-done | bytes 77856 | tf_op jit(solution)/shard_map/ppermute | solution.py:25
  30.9 0.0 copy-done
  30.9 0.7 %route.1 = (bf16[288,128]{1,0:T(8,128)(2,1)S(1)}, bf16[288,128]{1,0:T(8,128)(2,1)S(1)}, bf16[288,128]{1,0:T(8,128)(2,1)S(1)}, bf16[288,128]{1,0:T(8,128)(2,1)S(1...) custom-call(s32[2]{0:T(128)S(1)} %pad_add_fusion.here, ...), custom_call_target="tpu_custom_call" | custom-call | flops 268435456 | bytes 1048576 | tf_op jit(solution)/shard_map/route/pallas_call | solution.py:181
  31.6 3.4 %collective-permute-start.9 = (bf16[288,128]{1,0:T(8,128)(2,1)S(1)}, bf16[288,128]{1,0:T(8,128)(2,1)S(1)}, u32[]{:S(2)}, u32[]{:S(2)}) collective-permute-start(bf16[288,128]{1,0:T(8,128)(2,1)S(1)} %get-tuple-element.34), channel_id=1, source_target_pairs={{0,6},{1,7},{2,4},{3,5},{4,2},{5,3},{6,0},{7,1},{8,14},{9,15},{10,... | collective-permute-start | bytes 221192 | tf_op jit(solution)/shard_map/ppermute | solution.py:25
  35.0 0.0 collective-permute-start.10
  35.0 1.2 %collective-permute-start.11 = (bf16[288,128]{1,0:T(8,128)(2,1)S(1)}, bf16[288,128]{1,0:T(8,128)(2,1)S(1)}, u32[]{:S(2)}, u32[]{:S(2)}) collective-permute-start(bf16[288,128]{1,0:T(8,128)(2,1)S(1)} %get-tuple-element.36), channel_id=1, source_target_pairs={{0,7},{1,6},{2,5},{3,4},{4,3},{5,2},{6,1},{7,0},{8,15},{9,14},{10,... | collective-permute-start | bytes 221192 | tf_op jit(solution)/shard_map/ppermute | solution.py:25
  36.2 2.6 %collective-permute-start.12 = (bf16[288,128]{1,0:T(8,128)(2,1)S(1)}, bf16[288,128]{1,0:T(8,128)(2,1)S(1)}, u32[]{:S(2)}, u32[]{:S(2)}) collective-permute-start(bf16[288,128]{1,0:T(8,128)(2,1)S(1)} %get-tuple-element.37), channel_id=1, source_target_pairs={{0,5},{1,4},{2,7},{3,6},{4,1},{5,0},{6,3},{7,2},{8,13},{9,12},{10,... | collective-permute-start | bytes 221192 | tf_op jit(solution)/shard_map/ppermute | solution.py:25
  38.8 2.4 %collective-permute-start.13 = (bf16[288,128]{1,0:T(8,128)(2,1)S(1)}, bf16[288,128]{1,0:T(8,128)(2,1)S(1)}, u32[]{:S(2)}, u32[]{:S(2)}) collective-permute-start(bf16[288,128]{1,0:T(8,128)(2,1)S(1)} %get-tuple-element.38), channel_id=1, source_target_pairs={{0,3},{1,2},{2,1},{3,0},{4,7},{5,6},{6,5},{7,4},{8,11},{9,10},{10,... | collective-permute-start | bytes 221192 | tf_op jit(solution)/shard_map/ppermute | solution.py:25
  41.1 0.0 collective-permute-done.9.refs_1_
  41.1 1.1 %collective-permute-start.14 = (bf16[288,128]{1,0:T(8,128)(2,1)S(1)}, bf16[288,128]{1,0:T(8,128)(2,1)S(1)}, u32[]{:S(2)}, u32[]{:S(2)}) collective-permute-start(bf16[288,128]{1,0:T(8,128)(2,1)S(1)} %get-tuple-element.39), channel_id=1, source_target_pairs={{0,2},{1,3},{2,0},{3,1},{4,6},{5,7},{6,4},{7,5},{8,10},{9,11},{10,... | collective-permute-start | bytes 221192 | tf_op jit(solution)/shard_map/ppermute | solution.py:25
  42.2 2.5 %collective-permute-done.10.refs_2_ = bf16[288,128]{1,0:T(8,128)(2,1)S(1)} collective-permute-done((bf16[288,128]{1,0:T(8,128)(2,1)S(1)}, bf16[288,128]{1,0:T(8,128)(2,1)S(1)}, u32[]{:S(2)}, u32[]{:S(2)}) %collective-permute-start.10) | collective-permute-done | bytes 73760 | tf_op jit(solution)/shard_map/ppermute | solution.py:25
  44.7 1.4 %collective-permute-start.15 = (bf16[288,128]{1,0:T(8,128)(2,1)S(1)}, bf16[288,128]{1,0:T(8,128)(2,1)S(1)}, u32[]{:S(2)}, u32[]{:S(2)}) collective-permute-start(bf16[288,128]{1,0:T(8,128)(2,1)S(1)} %get-tuple-element.40), channel_id=1, source_target_pairs={{0,1},{1,0},{2,3},{3,2},{4,5},{5,4},{6,7},{7,6},{8,9},{9,8},{10,11... | collective-permute-start | bytes 221192 | tf_op jit(solution)/shard_map/ppermute | solution.py:25
  46.1 0.0 collective-permute-done.11.refs_3_
  46.1 1.5 %collective-permute-done.12.refs_4_ = bf16[288,128]{1,0:T(8,128)(2,1)S(1)} collective-permute-done((bf16[288,128]{1,0:T(8,128)(2,1)S(1)}, bf16[288,128]{1,0:T(8,128)(2,1)S(1)}, u32[]{:S(2)}, u32[]{:S(2)}) %collective-permute-start.12) | collective-permute-done | bytes 73760 | tf_op jit(solution)/shard_map/ppermute | solution.py:25
  47.6 0.0 collective-permute-done.13.refs_5_
  47.6 0.0 collective-permute-done.14.refs_6_
  47.6 1.4 %collective-permute-done.15.refs_7_ = bf16[288,128]{1,0:T(8,128)(2,1)S(1)} collective-permute-done((bf16[288,128]{1,0:T(8,128)(2,1)S(1)}, bf16[288,128]{1,0:T(8,128)(2,1)S(1)}, u32[]{:S(2)}, u32[]{:S(2)}) %collective-permute-start.15) | collective-permute-done | bytes 73760 | tf_op jit(solution)/shard_map/ppermute | solution.py:25
  49.0 0.6 %share.1 = (bf16[2,6,32,128]{3,2,1,0:T(8,128)(2,1)S(1)}, bf16[2,6,32,128]{3,2,1,0:T(8,128)(2,1)S(1)}, bf16[2,6,32,128]{3,2,1,0:T(8,128)(2,1)S(1)}, bf16[2,6,32,128]{3,2,1,0:T(8,128)(2,1)S(1)}) custom-call(s32[2]{0:T(128)S(1)} %pad_add_fusion.here, bf16[288,128]{1,0:T(8,128)(2,1)S(1)} %get-tuple-element.33.refs_0_, ...), custom_call_target="tpu_custom_call" | custom-call | flops 268435456 | bytes 1048576 | tf_op jit(solution)/shard_map/share/pallas_call | solution.py:187
  49.6 0.1 collective-permute-start.16
  49.8 0.0 collective-permute-start.17
  49.8 2.0 %collective-permute-start.18 = (bf16[2,6,32,128]{3,2,1,0:T(8,128)(2,1)S(1)}, bf16[2,6,32,128]{3,2,1,0:T(8,128)(2,1)S(1)}, u32[]{:S(2)}, u32[]{:S(2)}) collective-permute-start(bf16[2,6,32,128]{3,2,1,0:T(8,128)(2,1)S(1)} %get-tuple-element.46), channel_id=1, source_target_pairs={{0,8},{8,0},{16,24},{24,16},{1,9},{9,1},{17,25},{25,17},{2,10},{10... | collective-permute-start | bytes 294920 | tf_op jit(solution)/shard_map/ppermute | solution.py:25
  51.9 1.4 %join.1 = (bf16[1,6,128,128]{3,2,1,0:T(8,128)(2,1)}, bf16[2,1,6,128,128]{4,3,2,1,0:T(8,128)(2,1)}) custom-call(s32[2]{0:T(128)S(1)} %pad_add_fusion.here, bf16[288,128]{1,0:T(8,128)(2,1)S(1)} %get-tuple-element.33.refs_0_, bf16[288,128]{1,0:T(8,128)(2,1)S(1)} %collective-permute-done.9.refs_1_, bf16[288,128]{1,0:T(8,128)(2,1)S(1)} %collective-permute-done.10.refs_2_, ...), custom_call_target="tpu_custom_call" | custom-call | flops 268435456 | bytes 1048576 | tf_op jit(solution)/shard_map/join/pallas_call | solution.py:190
  53.3 1.6 %collective-permute-done.16 = bf16[2,6,32,128]{3,2,1,0:T(8,128)(2,1)S(1)} collective-permute-done((bf16[2,6,32,128]{3,2,1,0:T(8,128)(2,1)S(1)}, bf16[2,6,32,128]{3,2,1,0:T(8,128)(2,1)S(1)}, u32[]{:S(2)}, u32[]{:S(2)}) %collective-permute-start.16) | collective-permute-done | bytes 98336 | tf_op jit(solution)/shard_map/ppermute | solution.py:25
  54.9 0.0 collective-permute-done.17
  54.9 0.0 collective-permute-done.18
  54.9 0.7 %convert_add_fusion = f32[2,6,32,128]{3,2,1,0:T(8,128)} fusion(bf16[2,6,32,128]{3,2,1,0:T(8,128)(2,1)S(1)} %collective-permute-done.18, bf16[2,6,32,128]{3,2,1,0:T(8,128)(2,1)S(1)} %collective-permute-done.17, bf16[2,6,32,128]{3,2,1,0:T(8,128)(2,1)S(1)} %collective-permute-done.16, bf16[2,6,32,128]{3,2,1,0:T(8,128)(2,1)S(1)} %get-tuple-element.43), kind=kLoop, calls=%fused_computation | loop fusion | flops 344064 | bytes 589824 | tf_op jit(solution)/shard_map/add | solution.py:229
Async XLA Ops:
  0.6 10.2 %collective-permute-start.1 = (bf16[2,1,6,128,128]{4,3,2,1,0:T(8,128)(2,1)}, bf16[2,1,6,128,128]{4,3,2,1,0:T(8,128)(2,1)S(1)}, u32[]{:S(2)}, u32[]{:S(2)}) collective-permute-start(bf16[2,1,6,128,128]{4,3,2,1,0:T(8,128)(2,1)} %param.8), channel_id=1, source_target_pairs={{0,8},{8,16},{16,24},{24,0},{1,9},{9,17},{17,25},{25,1},{2,10},{10... | collective-permute-start | bytes 1179656 | tf_op jit(solution)/shard_map/ppermute | solution.py:223
  1.1 9.7 %collective-permute-start = (bf16[1,6,128,128]{3,2,1,0:T(8,128)(2,1)}, bf16[1,6,128,128]{3,2,1,0:T(8,128)(2,1)S(1)}, u32[]{:S(2)}, u32[]{:S(2)}) collective-permute-start(bf16[1,6,128,128]{3,2,1,0:T(8,128)(2,1)} %param.7), channel_id=1, source_target_pairs={{0,8},{8,16},{16,24},{24,0},{1,9},{9,17},{17,25},{25,1},{2,10},{10... | collective-permute-start | bytes 589832 | tf_op jit(solution)/shard_map/ppermute | solution.py:222
  4.6 26.2 %copy-start = (s32[1,48]{1,0:T(1,128)S(1)}, s32[1,48]{1,0:T(1,128)}, u32[]{:S(2)}) copy-start(s32[1,48]{1,0:T(1,128)} %joining.1) | copy-start | bytes 580
  11.9 10.7 %collective-permute-start.2 = (bf16[304,128]{1,0:T(8,128)(2,1)S(1)}, bf16[304,128]{1,0:T(8,128)(2,1)S(1)}, u32[]{:S(2)}, u32[]{:S(2)}) collective-permute-start(bf16[304,128]{1,0:T(8,128)(2,1)S(1)} %get-tuple-element.26), channel_id=1, source_target_pairs={{0,6},{1,7},{2,4},{3,5},{4,2},{5,3},{6,0},{7,1},{8,14},{9,15},{10,... | collective-permute-start | bytes 233480 | tf_op jit(solution)/shard_map/ppermute | solution.py:25
  16.3 8.9 %collective-permute-start.3 = (bf16[304,128]{1,0:T(8,128)(2,1)S(1)}, bf16[304,128]{1,0:T(8,128)(2,1)S(1)}, u32[]{:S(2)}, u32[]{:S(2)}) collective-permute-start(bf16[304,128]{1,0:T(8,128)(2,1)S(1)} %get-tuple-element.27), channel_id=1, source_target_pairs={{0,4},{1,5},{2,6},{3,7},{4,0},{5,1},{6,2},{7,3},{8,12},{9,13},{10,... | collective-permute-start | bytes 233480 | tf_op jit(solution)/shard_map/ppermute | solution.py:25
  16.3 10.4 %collective-permute-start.4 = (bf16[304,128]{1,0:T(8,128)(2,1)S(1)}, bf16[304,128]{1,0:T(8,128)(2,1)S(1)}, u32[]{:S(2)}, u32[]{:S(2)}) collective-permute-start(bf16[304,128]{1,0:T(8,128)(2,1)S(1)} %get-tuple-element.28), channel_id=1, source_target_pairs={{0,7},{1,6},{2,5},{3,4},{4,3},{5,2},{6,1},{7,0},{8,15},{9,14},{10,... | collective-permute-start | bytes 233480 | tf_op jit(solution)/shard_map/ppermute | solution.py:25
  19.2 10.9 %collective-permute-start.5 = (bf16[304,128]{1,0:T(8,128)(2,1)S(1)}, bf16[304,128]{1,0:T(8,128)(2,1)S(1)}, u32[]{:S(2)}, u32[]{:S(2)}) collective-permute-start(bf16[304,128]{1,0:T(8,128)(2,1)S(1)} %get-tuple-element.29), channel_id=1, source_target_pairs={{0,5},{1,4},{2,7},{3,6},{4,1},{5,0},{6,3},{7,2},{8,13},{9,12},{10,... | collective-permute-start | bytes 233480 | tf_op jit(solution)/shard_map/ppermute | solution.py:25
  20.2 9.9 %collective-permute-start.6 = (bf16[304,128]{1,0:T(8,128)(2,1)S(1)}, bf16[304,128]{1,0:T(8,128)(2,1)S(1)}, u32[]{:S(2)}, u32[]{:S(2)}) collective-permute-start(bf16[304,128]{1,0:T(8,128)(2,1)S(1)} %get-tuple-element.30), channel_id=1, source_target_pairs={{0,3},{1,2},{2,1},{3,0},{4,7},{5,6},{6,5},{7,4},{8,11},{9,10},{10,... | collective-permute-start | bytes 233480 | tf_op jit(solution)/shard_map/ppermute | solution.py:25
  22.6 7.6 %collective-permute-start.7 = (bf16[304,128]{1,0:T(8,128)(2,1)S(1)}, bf16[304,128]{1,0:T(8,128)(2,1)S(1)}, u32[]{:S(2)}, u32[]{:S(2)}) collective-permute-start(bf16[304,128]{1,0:T(8,128)(2,1)S(1)} %get-tuple-element.31), channel_id=1, source_target_pairs={{0,2},{1,3},{2,0},{3,1},{4,6},{5,7},{6,4},{7,5},{8,10},{9,11},{10,... | collective-permute-start | bytes 233480 | tf_op jit(solution)/shard_map/ppermute | solution.py:25
  25.3 5.6 %collective-permute-start.8 = (bf16[304,128]{1,0:T(8,128)(2,1)S(1)}, bf16[304,128]{1,0:T(8,128)(2,1)S(1)}, u32[]{:S(2)}, u32[]{:S(2)}) collective-permute-start(bf16[304,128]{1,0:T(8,128)(2,1)S(1)} %get-tuple-element.32), channel_id=1, source_target_pairs={{0,1},{1,0},{2,3},{3,2},{4,5},{5,4},{6,7},{7,6},{8,9},{9,8},{10,11... | collective-permute-start | bytes 233480 | tf_op jit(solution)/shard_map/ppermute | solution.py:25
  31.6 9.6 %collective-permute-start.9 = (bf16[288,128]{1,0:T(8,128)(2,1)S(1)}, bf16[288,128]{1,0:T(8,128)(2,1)S(1)}, u32[]{:S(2)}, u32[]{:S(2)}) collective-permute-start(bf16[288,128]{1,0:T(8,128)(2,1)S(1)} %get-tuple-element.34), channel_id=1, source_target_pairs={{0,6},{1,7},{2,4},{3,5},{4,2},{5,3},{6,0},{7,1},{8,14},{9,15},{10,... | collective-permute-start | bytes 221192 | tf_op jit(solution)/shard_map/ppermute | solution.py:25
  35.0 9.7 %collective-permute-start.10 = (bf16[288,128]{1,0:T(8,128)(2,1)S(1)}, bf16[288,128]{1,0:T(8,128)(2,1)S(1)}, u32[]{:S(2)}, u32[]{:S(2)}) collective-permute-start(bf16[288,128]{1,0:T(8,128)(2,1)S(1)} %get-tuple-element.35), channel_id=1, source_target_pairs={{0,4},{1,5},{2,6},{3,7},{4,0},{5,1},{6,2},{7,3},{8,12},{9,13},{10,... | collective-permute-start | bytes 221192 | tf_op jit(solution)/shard_map/ppermute | solution.py:25
  35.0 11.1 %collective-permute-start.11 = (bf16[288,128]{1,0:T(8,128)(2,1)S(1)}, bf16[288,128]{1,0:T(8,128)(2,1)S(1)}, u32[]{:S(2)}, u32[]{:S(2)}) collective-permute-start(bf16[288,128]{1,0:T(8,128)(2,1)S(1)} %get-tuple-element.36), channel_id=1, source_target_pairs={{0,7},{1,6},{2,5},{3,4},{4,3},{5,2},{6,1},{7,0},{8,15},{9,14},{10,... | collective-permute-start | bytes 221192 | tf_op jit(solution)/shard_map/ppermute | solution.py:25
  36.2 11.4 %collective-permute-start.12 = (bf16[288,128]{1,0:T(8,128)(2,1)S(1)}, bf16[288,128]{1,0:T(8,128)(2,1)S(1)}, u32[]{:S(2)}, u32[]{:S(2)}) collective-permute-start(bf16[288,128]{1,0:T(8,128)(2,1)S(1)} %get-tuple-element.37), channel_id=1, source_target_pairs={{0,5},{1,4},{2,7},{3,6},{4,1},{5,0},{6,3},{7,2},{8,13},{9,12},{10,... | collective-permute-start | bytes 221192 | tf_op jit(solution)/shard_map/ppermute | solution.py:25
  38.8 8.8 %collective-permute-start.13 = (bf16[288,128]{1,0:T(8,128)(2,1)S(1)}, bf16[288,128]{1,0:T(8,128)(2,1)S(1)}, u32[]{:S(2)}, u32[]{:S(2)}) collective-permute-start(bf16[288,128]{1,0:T(8,128)(2,1)S(1)} %get-tuple-element.38), channel_id=1, source_target_pairs={{0,3},{1,2},{2,1},{3,0},{4,7},{5,6},{6,5},{7,4},{8,11},{9,10},{10,... | collective-permute-start | bytes 221192 | tf_op jit(solution)/shard_map/ppermute | solution.py:25
  41.1 6.5 %collective-permute-start.14 = (bf16[288,128]{1,0:T(8,128)(2,1)S(1)}, bf16[288,128]{1,0:T(8,128)(2,1)S(1)}, u32[]{:S(2)}, u32[]{:S(2)}) collective-permute-start(bf16[288,128]{1,0:T(8,128)(2,1)S(1)} %get-tuple-element.39), channel_id=1, source_target_pairs={{0,2},{1,3},{2,0},{3,1},{4,6},{5,7},{6,4},{7,5},{8,10},{9,11},{10,... | collective-permute-start | bytes 221192 | tf_op jit(solution)/shard_map/ppermute | solution.py:25
  44.7 4.4 %collective-permute-start.15 = (bf16[288,128]{1,0:T(8,128)(2,1)S(1)}, bf16[288,128]{1,0:T(8,128)(2,1)S(1)}, u32[]{:S(2)}, u32[]{:S(2)}) collective-permute-start(bf16[288,128]{1,0:T(8,128)(2,1)S(1)} %get-tuple-element.40), channel_id=1, source_target_pairs={{0,1},{1,0},{2,3},{3,2},{4,5},{5,4},{6,7},{7,6},{8,9},{9,8},{10,11... | collective-permute-start | bytes 221192 | tf_op jit(solution)/shard_map/ppermute | solution.py:25
  49.6 5.2 %collective-permute-start.16 = (bf16[2,6,32,128]{3,2,1,0:T(8,128)(2,1)S(1)}, bf16[2,6,32,128]{3,2,1,0:T(8,128)(2,1)S(1)}, u32[]{:S(2)}, u32[]{:S(2)}) collective-permute-start(bf16[2,6,32,128]{3,2,1,0:T(8,128)(2,1)S(1)} %get-tuple-element.44), channel_id=1, source_target_pairs={{0,16},{8,24},{16,0},{24,8},{1,17},{9,25},{17,1},{25,9},{2,18},{10... | collective-permute-start | bytes 294920 | tf_op jit(solution)/shard_map/ppermute | solution.py:25
  49.8 5.1 %collective-permute-start.17 = (bf16[2,6,32,128]{3,2,1,0:T(8,128)(2,1)S(1)}, bf16[2,6,32,128]{3,2,1,0:T(8,128)(2,1)S(1)}, u32[]{:S(2)}, u32[]{:S(2)}) collective-permute-start(bf16[2,6,32,128]{3,2,1,0:T(8,128)(2,1)S(1)} %get-tuple-element.45), channel_id=1, source_target_pairs={{0,24},{8,16},{16,8},{24,0},{1,25},{9,17},{17,9},{25,1},{2,26},{10... | collective-permute-start | bytes 294920 | tf_op jit(solution)/shard_map/ppermute | solution.py:25
  49.8 5.1 %collective-permute-start.18 = (bf16[2,6,32,128]{3,2,1,0:T(8,128)(2,1)S(1)}, bf16[2,6,32,128]{3,2,1,0:T(8,128)(2,1)S(1)}, u32[]{:S(2)}, u32[]{:S(2)}) collective-permute-start(bf16[2,6,32,128]{3,2,1,0:T(8,128)(2,1)S(1)} %get-tuple-element.46), channel_id=1, source_target_pairs={{0,8},{8,0},{16,24},{24,16},{1,9},{9,1},{17,25},{25,17},{2,10},{10... | collective-permute-start | bytes 294920 | tf_op jit(solution)/shard_map/ppermute | solution.py:25

commit v3 on v2

--- a/solution.py
+++ b/solution.py
@@ -129,10 +129,10 @@
             out[p][i * size : (i + 1) * size] = (held[q].astype(jnp.float32) / divisor).astype(jnp.bfloat16)
 
 
-def share_kernel(steps, site_steps, here, *refs):
-    n, sites = len(steps), len(site_steps)
-    pieces, shares, stage = refs[:n], refs[n : n + sites], refs[n + sites]
-    _, slots, wide, m = shares[0].shape
+def share_kernel(steps, here, *refs):
+    n = len(steps)
+    pieces, kept, away, stage = refs[:n], refs[n], refs[n + 1], refs[n + 2]
+    _, _, slots, wide, m = kept.shape
     rows = m // n
     for p, k in enumerate(steps):
         first = pl.multiple_of(jnp.bitwise_xor(here[0], k) * rows, rows)
@@ -140,11 +140,11 @@
             for c in range(2):
                 at = (3 * i + 1 + c) * rows
                 stage[c, i, pl.ds(first, rows)] = pieces[p][at : at + rows]
-    for p, k in enumerate(site_steps):
+    for out, place, k in ((away, 0, 1), (away, 1, 3), (kept, 0, 0), (kept, 1, 2)):
         first = pl.multiple_of(jnp.bitwise_xor(here[1], k) * wide, wide)
         for i in range(slots):
             for c in range(2):
-                shares[p][c, i] = stage[c, i, pl.ds(first, wide)]
+                out[place, c, i] = stage[c, i, pl.ds(first, wide)]
 
 
 def join_kernel(steps, here, *refs):
@@ -168,7 +168,7 @@
     shape = lambda *dims: jax.ShapeDtypeStruct(dims, jnp.bfloat16)
     scratch = lambda *dims: [pltpu.VMEM(dims, jnp.bfloat16)]
     bind = functools.partial
-    steps, site_steps = far_first(n), far_first(sites)
+    steps = far_first(n)
     here = jnp.stack([lax.axis_index("blk"), lax.axis_index("site")]).astype(jnp.int32)
     pieces = [shape(3 * slots * rows + TILE, m)] * n
     kept = scratch(3 * slots, m, m)
@@ -183,12 +183,14 @@
     )
     parts = all_swapped(parts, steps, "blk")
     ins = [SMEM] + [VMEM] * n
-    pieces = [shape(2, slots, m // sites, m)] * sites
-    shares = small_call(bind(share_kernel, steps, site_steps), pieces, ins, scratch(2, slots, m, m), "share")(here, *parts)
-    shares = all_swapped(shares, site_steps, "site")
+    pieces = [shape(2, 2, slots, m // sites, m)] * 2
+    kept, away = small_call(bind(share_kernel, steps), pieces, ins, scratch(2, slots, m, m), "share")(here, *parts)
+    came = lax.ppermute(away, "site", [(i, i ^ 1) for i in range(sites)])
+    partial = kept.astype(jnp.float32) + came.astype(jnp.float32)
+    came = lax.ppermute(partial[1].astype(jnp.bfloat16), "site", [(i, i ^ 2) for i in range(sites)])
     pieces = [shape(1, slots, m, m), shape(2, 1, slots, m, m)]
     new_corner, new_b = small_call(bind(join_kernel, steps), pieces, ins, [], "join")(here, *parts)
-    return new_corner, new_b, shares
+    return new_corner, new_b, partial[0] + came.astype(jnp.float32)
 
 
 def transposed(pieces):
@@ -210,7 +212,7 @@
     new = jnp.transpose(final, (2, 1, 0, 3, 4)).reshape(3, slots, m, m)
     shares = jnp.moveaxis(new[1:].reshape(2, slots, sites, m // sites, m), 2, 0)
     shares = lax.all_to_all(shares, "site", 0, 0, tiled=True)
-    return new[0][None], new[1:][:, None], [shares[i] for i in range(sites)]
+    return new[0][None], new[1:][:, None], jnp.sum(shares.astype(jnp.float32), axis=0)
 
 
 def per_device(corner, bcorner, edge, bedge, proj, joining, momentum):
@@ -219,15 +221,12 @@
     angle = momentum[0] * lax.axis_index("site").astype(jnp.float32)
     turn = jnp.stack([jnp.cos(angle), jnp.sin(angle)])
     onward = [(i, (i + 1) % sites) for i in range(sites)]
-    left_corner = lax.ppermute(corner, "site", onward)
     left_bcorner = lax.ppermute(bcorner, "site", onward)
+    left_corner = lax.ppermute(corner, "site", [(i, i ^ 1) for i in range(sites)])
+    left_corner = lax.ppermute(left_corner, "site", [(i, i if i % 2 else (i + 2) % sites) for i in range(sites)])
     wv = edge_proj(edge, bedge, proj)
-    routed = routed_by_tiles if m % (n * TILE) == 0 and m % (sites * TILE) == 0 else routed_by_rows
-    new_corner, new_b, shares = routed(turn, left_corner, left_bcorner, wv, joining, n, sites)
-    summed = shares[0].astype(jnp.float32)
-    for share in shares[1:]:
-        summed = summed + share.astype(jnp.float32)
-    return (new_corner, new_b, summed)
+    routed = routed_by_tiles if m % (n * TILE) == 0 and sites == 4 else routed_by_rows
+    return routed(turn, left_corner, left_bcorner, wv, joining, n, sites)
 
 
 def solution(mesh):

time: 56.2 us -> 56.5 us (level)
  waiting for transfers between devices: 12.3 us -> 16.2 us
  starting transfers between devices: 31.9 us -> 28.7 us
    ppermute x17 -> x14, starting transfers between devices: 28.8 us -> 22.5 us  [all_swapped(): lax.ppermute(part, axis, [(i, i ^ k) for i in range(n)])]
    ppermute x1 -> x4, waiting for transfers between devices: 0.84 us -> 4.51 us  [the longest x1 2.75 us: routed_by_tiles(): lax.ppermute(partial[1].astype(jnp.bfloat16), 'site', [(i, i ^ 2) for i i...]
    ppermute x1 -> x4, starting transfers between devices: 2.63 us -> 6.11 us  [the longest x1 4.78 us: per_device(): lax.ppermute(left_corner, 'site', [(i, i if i % 2 else (i + 2) % sites) f...]
    ppermute x17 -> x14, waiting for transfers between devices: 11.5 us -> 11.7 us  [all_swapped(): lax.ppermute(part, axis, [(i, i ^ k) for i in range(n)])]
  transfers between devices with their start and end apart: 19 -> 19, of which waited for: 8 -> 9; matrix products, arithmetic and copies ran while one was open for 0% -> 0% of each run, Pallas kernels for 12% -> 12%
where the time goes in v3:
time: 56.5 us; the launch traced here: 56.3 us
  starting transfers between devices  28.7 us (51%)
  waiting for transfers between devices  16.2 us (29%)
  Pallas kernels  9 us (16%)
  between operations  1.52 us (3%)
  other arithmetic  0.9 us (2%)
    ppermute x14, starting transfers between devices, all_swapped(): lax.ppermute(part, axis, [(i, i ^ k) for i in range(n)])  22.5 us
    ppermute x14, waiting for transfers between devices, all_swapped(): lax.ppermute(part, axis, [(i, i ^ k) for i in range(n)])  11.7 us
    pallas_call x1, Pallas kernels, edge_proj(): pl.pallas_call(edge_proj_kernel, out_shape=jax.ShapeDtypeStruct((2 * slot...  5.28 us
    ppermute x1, starting transfers between devices, per_device(): lax.ppermute(left_corner, 'site', [(i, i if i % 2 else (i + 2) % sites) f...  4.78 us
    ppermute x1, waiting for transfers between devices, routed_by_tiles(): lax.ppermute(partial[1].astype(jnp.bfloat16), 'site', [(i, i ^ 2) for i i...  2.75 us
    ppermute x1, waiting for transfers between devices, routed_by_tiles(): came = lax.ppermute(away, 'site', [(i, i ^ 1) for i in range(sites)])  1.43 us
    pallas_call x1, Pallas kernels, routed_by_tiles(): small_call(bind(join_kernel, steps), pieces, ins, [], 'join')(here, *parts)  1.42 us
  transfers between devices with their start and end apart: 19, of which 9 were waited for; matrix products, arithmetic and copies ran while one was open for 0% of the time, Pallas kernels for 12%

profile of v3, /device:TPU:0, one launch (start us, length us, event | category | flops | bytes accessed | tf_op | source)
XLA Modules:
  0.0 56.3 jit_solution(2514670238952325057)
XLA Ops:
  0.6 0.5 collective-permute-start
  1.1 0.1 collective-permute-start.2
  2.0 0.1 pad_add_fusion.here
  2.1 0.0 copy-start
  2.1 0.3 collective-permute-done
  2.4 4.8 %collective-permute-start.1 = (bf16[1,6,128,128]{3,2,1,0:T(8,128)(2,1)S(1)}, bf16[1,6,128,128]{3,2,1,0:T(8,128)(2,1)S(1)}, u32[]{:S(2)}, u32[]{:S(2)}) collective-permute-start(bf16[1,6,128,128]{3,2,1,0:T(8,128)(2,1)S(1)} %collective-permute-done), channel_id=1, source_target_pairs={{0,16},{8,8},{16,0},{24,24},{1,17},{9,9},{17,1},{25,25},{2,18},{10... | collective-permute-start | bytes 589832 | tf_op jit(solution)/shard_map/ppermute | solution.py:226
  7.2 5.3 %edge_proj.1.wv = bf16[12,128,128]{2,1,0:T(8,128)(2,1)S(1)} custom-call(bf16[1,6,128,2304]{3,2,1,0:T(8,128)(2,1)} %edge.1, bf16[1,6,128,2304]{3,2,1,0:T(8,128)(2,1)} %bedge.1, bf16[1,6,2304,128]{3,2,1,0:T(8,128)(2,1)} %proj.1), custom_call_target="tpu_custom_call" | custom-call | flops 905969664 | bytes 10616832 | tf_op jit(solution)/shard_map/edge_proj/pallas_call | solution.py:52
  12.5 0.1 pad_maximum_fusion.turn
  12.6 0.0 collective-permute-done.1.corner
  12.6 0.0 collective-permute-done.2.bcorner
  12.6 1.0 %spread.1 = (bf16[304,128]{1,0:T(8,128)(2,1)S(1)}, bf16[304,128]{1,0:T(8,128)(2,1)S(1)}, bf16[304,128]{1,0:T(8,128)(2,1)S(1)}, bf16[304,128]{1,0:T(8,128)(2,1)S(...) custom-call(s32[2]{0:T(128)S(1)} %pad_add_fusion.here, ...), custom_call_target="tpu_custom_call" | custom-call | flops 268435456 | bytes 1048576 | tf_op jit(solution)/shard_map/spread/pallas_call | solution.py:175
  13.6 3.7 %collective-permute-start.3 = (bf16[304,128]{1,0:T(8,128)(2,1)S(1)}, bf16[304,128]{1,0:T(8,128)(2,1)S(1)}, u32[]{:S(2)}, u32[]{:S(2)}) collective-permute-start(bf16[304,128]{1,0:T(8,128)(2,1)S(1)} %get-tuple-element.24), channel_id=1, source_target_pairs={{0,6},{1,7},{2,4},{3,5},{4,2},{5,3},{6,0},{7,1},{8,14},{9,15},{10,... | collective-permute-start | bytes 233480 | tf_op jit(solution)/shard_map/ppermute | solution.py:25
  17.3 0.0 collective-permute-start.4
  17.3 2.8 %collective-permute-start.5 = (bf16[304,128]{1,0:T(8,128)(2,1)S(1)}, bf16[304,128]{1,0:T(8,128)(2,1)S(1)}, u32[]{:S(2)}, u32[]{:S(2)}) collective-permute-start(bf16[304,128]{1,0:T(8,128)(2,1)S(1)} %get-tuple-element.26), channel_id=1, source_target_pairs={{0,7},{1,6},{2,5},{3,4},{4,3},{5,2},{6,1},{7,0},{8,15},{9,14},{10,... | collective-permute-start | bytes 233480 | tf_op jit(solution)/shard_map/ppermute | solution.py:25
  20.1 1.0 %collective-permute-start.6 = (bf16[304,128]{1,0:T(8,128)(2,1)S(1)}, bf16[304,128]{1,0:T(8,128)(2,1)S(1)}, u32[]{:S(2)}, u32[]{:S(2)}) collective-permute-start(bf16[304,128]{1,0:T(8,128)(2,1)S(1)} %get-tuple-element.27), channel_id=1, source_target_pairs={{0,5},{1,4},{2,7},{3,6},{4,1},{5,0},{6,3},{7,2},{8,13},{9,12},{10,... | collective-permute-start | bytes 233480 | tf_op jit(solution)/shard_map/ppermute | solution.py:25
  21.1 2.4 %collective-permute-start.7 = (bf16[304,128]{1,0:T(8,128)(2,1)S(1)}, bf16[304,128]{1,0:T(8,128)(2,1)S(1)}, u32[]{:S(2)}, u32[]{:S(2)}) collective-permute-start(bf16[304,128]{1,0:T(8,128)(2,1)S(1)} %get-tuple-element.28), channel_id=1, source_target_pairs={{0,3},{1,2},{2,1},{3,0},{4,7},{5,6},{6,5},{7,4},{8,11},{9,10},{10,... | collective-permute-start | bytes 233480 | tf_op jit(solution)/shard_map/ppermute | solution.py:25
  23.5 0.0 collective-permute-done.3.refs_1_
  23.5 0.5 collective-permute-start.8
  24.0 2.8 %collective-permute-done.4.refs_2_ = bf16[304,128]{1,0:T(8,128)(2,1)S(1)} collective-permute-done((bf16[304,128]{1,0:T(8,128)(2,1)S(1)}, bf16[304,128]{1,0:T(8,128)(2,1)S(1)}, u32[]{:S(2)}, u32[]{:S(2)}) %collective-permute-start.4) | collective-permute-done | bytes 77856 | tf_op jit(solution)/shard_map/ppermute | solution.py:25
  26.8 1.5 %collective-permute-start.9 = (bf16[304,128]{1,0:T(8,128)(2,1)S(1)}, bf16[304,128]{1,0:T(8,128)(2,1)S(1)}, u32[]{:S(2)}, u32[]{:S(2)}) collective-permute-start(bf16[304,128]{1,0:T(8,128)(2,1)S(1)} %get-tuple-element.30), channel_id=1, source_target_pairs={{0,1},{1,0},{2,3},{3,2},{4,5},{5,4},{6,7},{7,6},{8,9},{9,8},{10,11... | collective-permute-start | bytes 233480 | tf_op jit(solution)/shard_map/ppermute | solution.py:25
  28.3 0.0 collective-permute-done.5.refs_3_
  28.3 2.1 %collective-permute-done.6.refs_4_ = bf16[304,128]{1,0:T(8,128)(2,1)S(1)} collective-permute-done((bf16[304,128]{1,0:T(8,128)(2,1)S(1)}, bf16[304,128]{1,0:T(8,128)(2,1)S(1)}, u32[]{:S(2)}, u32[]{:S(2)}) %collective-permute-start.6) | collective-permute-done | bytes 77856 | tf_op jit(solution)/shard_map/ppermute | solution.py:25
  30.4 0.0 collective-permute-done.7.refs_5_
  30.4 0.0 collective-permute-done.8.refs_6_
  30.4 0.8 %collective-permute-done.9.refs_7_ = bf16[304,128]{1,0:T(8,128)(2,1)S(1)} collective-permute-done((bf16[304,128]{1,0:T(8,128)(2,1)S(1)}, bf16[304,128]{1,0:T(8,128)(2,1)S(1)}, u32[]{:S(2)}, u32[]{:S(2)}) %collective-permute-start.9) | collective-permute-done | bytes 77856 | tf_op jit(solution)/shard_map/ppermute | solution.py:25
  31.2 0.0 copy-done
  31.2 0.7 %route.1 = (bf16[288,128]{1,0:T(8,128)(2,1)S(1)}, bf16[288,128]{1,0:T(8,128)(2,1)S(1)}, bf16[288,128]{1,0:T(8,128)(2,1)S(1)}, bf16[288,128]{1,0:T(8,128)(2,1)S(1...) custom-call(s32[2]{0:T(128)S(1)} %pad_add_fusion.here, ...), custom_call_target="tpu_custom_call" | custom-call | flops 268435456 | bytes 1048576 | tf_op jit(solution)/shard_map/route/pallas_call | solution.py:181
  31.9 2.7 %collective-permute-start.10 = (bf16[288,128]{1,0:T(8,128)(2,1)S(1)}, bf16[288,128]{1,0:T(8,128)(2,1)S(1)}, u32[]{:S(2)}, u32[]{:S(2)}) collective-permute-start(bf16[288,128]{1,0:T(8,128)(2,1)S(1)} %get-tuple-element.32), channel_id=1, source_target_pairs={{0,6},{1,7},{2,4},{3,5},{4,2},{5,3},{6,0},{7,1},{8,14},{9,15},{10,... | collective-permute-start | bytes 221192 | tf_op jit(solution)/shard_map/ppermute | solution.py:25
  34.7 0.0 collective-permute-start.11
  34.7 2.0 %collective-permute-start.12 = (bf16[288,128]{1,0:T(8,128)(2,1)S(1)}, bf16[288,128]{1,0:T(8,128)(2,1)S(1)}, u32[]{:S(2)}, u32[]{:S(2)}) collective-permute-start(bf16[288,128]{1,0:T(8,128)(2,1)S(1)} %get-tuple-element.34), channel_id=1, source_target_pairs={{0,7},{1,6},{2,5},{3,4},{4,3},{5,2},{6,1},{7,0},{8,15},{9,14},{10,... | collective-permute-start | bytes 221192 | tf_op jit(solution)/shard_map/ppermute | solution.py:25
  36.7 2.4 %collective-permute-start.13 = (bf16[288,128]{1,0:T(8,128)(2,1)S(1)}, bf16[288,128]{1,0:T(8,128)(2,1)S(1)}, u32[]{:S(2)}, u32[]{:S(2)}) collective-permute-start(bf16[288,128]{1,0:T(8,128)(2,1)S(1)} %get-tuple-element.35), channel_id=1, source_target_pairs={{0,5},{1,4},{2,7},{3,6},{4,1},{5,0},{6,3},{7,2},{8,13},{9,12},{10,... | collective-permute-start | bytes 221192 | tf_op jit(solution)/shard_map/ppermute | solution.py:25
  39.1 2.4 %collective-permute-start.14 = (bf16[288,128]{1,0:T(8,128)(2,1)S(1)}, bf16[288,128]{1,0:T(8,128)(2,1)S(1)}, u32[]{:S(2)}, u32[]{:S(2)}) collective-permute-start(bf16[288,128]{1,0:T(8,128)(2,1)S(1)} %get-tuple-element.36), channel_id=1, source_target_pairs={{0,3},{1,2},{2,1},{3,0},{4,7},{5,6},{6,5},{7,4},{8,11},{9,10},{10,... | collective-permute-start | bytes 221192 | tf_op jit(solution)/shard_map/ppermute | solution.py:25
  41.4 0.0 collective-permute-done.10.refs_1_
  41.4 0.2 collective-permute-start.15
  41.7 2.5 %collective-permute-done.11.refs_2_ = bf16[288,128]{1,0:T(8,128)(2,1)S(1)} collective-permute-done((bf16[288,128]{1,0:T(8,128)(2,1)S(1)}, bf16[288,128]{1,0:T(8,128)(2,1)S(1)}, u32[]{:S(2)}, u32[]{:S(2)}) %collective-permute-start.11) | collective-permute-done | bytes 73760 | tf_op jit(solution)/shard_map/ppermute | solution.py:25
  44.1 0.9 %collective-permute-start.16 = (bf16[288,128]{1,0:T(8,128)(2,1)S(1)}, bf16[288,128]{1,0:T(8,128)(2,1)S(1)}, u32[]{:S(2)}, u32[]{:S(2)}) collective-permute-start(bf16[288,128]{1,0:T(8,128)(2,1)S(1)} %get-tuple-element.38), channel_id=1, source_target_pairs={{0,1},{1,0},{2,3},{3,2},{4,5},{5,4},{6,7},{7,6},{8,9},{9,8},{10,11... | collective-permute-start | bytes 221192 | tf_op jit(solution)/shard_map/ppermute | solution.py:25
  45.0 0.0 collective-permute-done.12.refs_3_
  45.0 2.3 %collective-permute-done.13.refs_4_ = bf16[288,128]{1,0:T(8,128)(2,1)S(1)} collective-permute-done((bf16[288,128]{1,0:T(8,128)(2,1)S(1)}, bf16[288,128]{1,0:T(8,128)(2,1)S(1)}, u32[]{:S(2)}, u32[]{:S(2)}) %collective-permute-start.13) | collective-permute-done | bytes 73760 | tf_op jit(solution)/shard_map/ppermute | solution.py:25
  47.3 0.0 collective-permute-done.14.refs_5_
  47.3 0.0 collective-permute-done.15.refs_6_
  47.4 1.1 %collective-permute-done.16.refs_7_ = bf16[288,128]{1,0:T(8,128)(2,1)S(1)} collective-permute-done((bf16[288,128]{1,0:T(8,128)(2,1)S(1)}, bf16[288,128]{1,0:T(8,128)(2,1)S(1)}, u32[]{:S(2)}, u32[]{:S(2)}) %collective-permute-start.16) | collective-permute-done | bytes 73760 | tf_op jit(solution)/shard_map/ppermute | solution.py:25
  48.5 0.6 %share.1 = (bf16[2,2,6,32,128]{4,3,2,1,0:T(8,128)(2,1)S(1)}, bf16[2,2,6,32,128]{4,3,2,1,0:T(8,128)(2,1)S(1)}) custom-call(s32[2]{0:T(128)S(1)} %pad_add_fusion.here, bf16[288,128]{1,0:T(8,128)(2,1)S(1)} %get-tuple-element.31.refs_0_, bf16[288,128]{1,0:T(8,128)(2,1)S(1)} %collective-permute-done.10.refs_1_, ...), custom_call_target="tpu_custom_call" | custom-call | flops 268435456 | bytes 1048576 | tf_op jit(solution)/shard_map/share/pallas_call | solution.py:187
  49.1 0.1 collective-permute-start.17
  49.2 1.4 %collective-permute-done.17 = bf16[2,2,6,32,128]{4,3,2,1,0:T(8,128)(2,1)S(1)} collective-permute-done((bf16[2,2,6,32,128]{4,3,2,1,0:T(8,128)(2,1)S(1)}, bf16[2,2,6,32,128]{4,3,2,1,0:T(8,128)(2,1)S(1)}, u32[]{:S(2)}, u32[]{:S(2)}) %collective-permute-start.17) | collective-permute-done | bytes 196640 | tf_op jit(solution)/shard_map/ppermute | solution.py:188
  50.7 0.7 %collective-permute-start.18 = (bf16[2,6,32,128]{3,2,1,0:T(8,128)(2,1)S(1)}, bf16[2,6,32,128]{3,2,1,0:T(8,128)(2,1)S(1)}, u32[]{:S(2)}, u32[]{:S(2)}) collective-permute-start(bf16[2,6,32,128]{3,2,1,0:T(8,128)(2,1)S(1)} %fusion.1), channel_id=1, source_target_pairs={{0,16},{8,24},{16,0},{24,8},{1,17},{9,25},{17,1},{25,9},{2,18},{10... | collective-permute-start | bytes 294920 | tf_op jit(solution)/shard_map/ppermute | solution.py:190
  51.4 1.4 %join.1 = (bf16[1,6,128,128]{3,2,1,0:T(8,128)(2,1)}, bf16[2,1,6,128,128]{4,3,2,1,0:T(8,128)(2,1)}) custom-call(s32[2]{0:T(128)S(1)} %pad_add_fusion.here, bf16[288,128]{1,0:T(8,128)(2,1)S(1)} %get-tuple-element.31.refs_0_, bf16[288,128]{1,0:T(8,128)(2,1)S(1)} %collective-permute-done.10.refs_1_, bf16[288,128]{1,0:T(8,128)(2,1)S(1)} %collective-permute-done.11.refs_2_, ...), custom_call_target="tpu_custom_call" | custom-call | flops 268435456 | bytes 1048576 | tf_op jit(solution)/shard_map/join/pallas_call | solution.py:192
  52.8 2.7 %collective-permute-done.18 = bf16[2,6,32,128]{3,2,1,0:T(8,128)(2,1)S(1)} collective-permute-done((bf16[2,6,32,128]{3,2,1,0:T(8,128)(2,1)S(1)}, bf16[2,6,32,128]{3,2,1,0:T(8,128)(2,1)S(1)}, u32[]{:S(2)}, u32[]{:S(2)}) %collective-permute-start.18) | collective-permute-done | bytes 98336 | tf_op jit(solution)/shard_map/ppermute | solution.py:190
  55.6 0.7 %fusion = f32[2,6,32,128]{3,2,1,0:T(8,128)} fusion(f32[2,2,6,32,128]{4,3,2,1,0:T(8,128)S(1)} %convert_add_fusion, bf16[2,6,32,128]{3,2,1,0:T(8,128)(2,1)S(1)} %collective-permute-done.18), kind=kLoop, calls=%fused_computation.3 | loop fusion | flops 98304 | bytes 491520 | tf_op jit(solution)/shard_map/add | solution.py:193
  (2 shorter events, 0.1 us)
Async XLA Ops:
  0.6 1.8 %collective-permute-start = (bf16[1,6,128,128]{3,2,1,0:T(8,128)(2,1)}, bf16[1,6,128,128]{3,2,1,0:T(8,128)(2,1)S(1)}, u32[]{:S(2)}, u32[]{:S(2)}) collective-permute-start(bf16[1,6,128,128]{3,2,1,0:T(8,128)(2,1)} %param.7), channel_id=1, source_target_pairs={{0,8},{8,0},{16,24},{24,16},{1,9},{9,1},{17,25},{25,17},{2,10},{10... | collective-permute-start | bytes 589832 | tf_op jit(solution)/shard_map/ppermute | solution.py:225
  1.1 11.4 %collective-permute-start.2 = (bf16[2,1,6,128,128]{4,3,2,1,0:T(8,128)(2,1)}, bf16[2,1,6,128,128]{4,3,2,1,0:T(8,128)(2,1)S(1)}, u32[]{:S(2)}, u32[]{:S(2)}) collective-permute-start(bf16[2,1,6,128,128]{4,3,2,1,0:T(8,128)(2,1)} %param.8), channel_id=1, source_target_pairs={{0,8},{8,16},{16,24},{24,0},{1,9},{9,17},{17,25},{25,1},{2,10},{10... | collective-permute-start | bytes 1179656 | tf_op jit(solution)/shard_map/ppermute | solution.py:224
  2.1 29.1 %copy-start = (s32[1,48]{1,0:T(1,128)S(1)}, s32[1,48]{1,0:T(1,128)}, u32[]{:S(2)}) copy-start(s32[1,48]{1,0:T(1,128)} %joining.1) | copy-start | bytes 580
  2.4 10.2 %collective-permute-start.1 = (bf16[1,6,128,128]{3,2,1,0:T(8,128)(2,1)S(1)}, bf16[1,6,128,128]{3,2,1,0:T(8,128)(2,1)S(1)}, u32[]{:S(2)}, u32[]{:S(2)}) collective-permute-start(bf16[1,6,128,128]{3,2,1,0:T(8,128)(2,1)S(1)} %collective-permute-done), channel_id=1, source_target_pairs={{0,16},{8,8},{16,0},{24,24},{1,17},{9,9},{17,1},{25,25},{2,18},{10... | collective-permute-start | bytes 589832 | tf_op jit(solution)/shard_map/ppermute | solution.py:226
  13.6 9.9 %collective-permute-start.3 = (bf16[304,128]{1,0:T(8,128)(2,1)S(1)}, bf16[304,128]{1,0:T(8,128)(2,1)S(1)}, u32[]{:S(2)}, u32[]{:S(2)}) collective-permute-start(bf16[304,128]{1,0:T(8,128)(2,1)S(1)} %get-tuple-element.24), channel_id=1, source_target_pairs={{0,6},{1,7},{2,4},{3,5},{4,2},{5,3},{6,0},{7,1},{8,14},{9,15},{10,... | collective-permute-start | bytes 233480 | tf_op jit(solution)/shard_map/ppermute | solution.py:25
  17.3 9.5 %collective-permute-start.4 = (bf16[304,128]{1,0:T(8,128)(2,1)S(1)}, bf16[304,128]{1,0:T(8,128)(2,1)S(1)}, u32[]{:S(2)}, u32[]{:S(2)}) collective-permute-start(bf16[304,128]{1,0:T(8,128)(2,1)S(1)} %get-tuple-element.25), channel_id=1, source_target_pairs={{0,4},{1,5},{2,6},{3,7},{4,0},{5,1},{6,2},{7,3},{8,12},{9,13},{10,... | collective-permute-start | bytes 233480 | tf_op jit(solution)/shard_map/ppermute | solution.py:25
  17.3 11.0 %collective-permute-start.5 = (bf16[304,128]{1,0:T(8,128)(2,1)S(1)}, bf16[304,128]{1,0:T(8,128)(2,1)S(1)}, u32[]{:S(2)}, u32[]{:S(2)}) collective-permute-start(bf16[304,128]{1,0:T(8,128)(2,1)S(1)} %get-tuple-element.26), channel_id=1, source_target_pairs={{0,7},{1,6},{2,5},{3,4},{4,3},{5,2},{6,1},{7,0},{8,15},{9,14},{10,... | collective-permute-start | bytes 233480 | tf_op jit(solution)/shard_map/ppermute | solution.py:25
  20.1 10.3 %collective-permute-start.6 = (bf16[304,128]{1,0:T(8,128)(2,1)S(1)}, bf16[304,128]{1,0:T(8,128)(2,1)S(1)}, u32[]{:S(2)}, u32[]{:S(2)}) collective-permute-start(bf16[304,128]{1,0:T(8,128)(2,1)S(1)} %get-tuple-element.27), channel_id=1, source_target_pairs={{0,5},{1,4},{2,7},{3,6},{4,1},{5,0},{6,3},{7,2},{8,13},{9,12},{10,... | collective-permute-start | bytes 233480 | tf_op jit(solution)/shard_map/ppermute | solution.py:25
  21.1 9.3 %collective-permute-start.7 = (bf16[304,128]{1,0:T(8,128)(2,1)S(1)}, bf16[304,128]{1,0:T(8,128)(2,1)S(1)}, u32[]{:S(2)}, u32[]{:S(2)}) collective-permute-start(bf16[304,128]{1,0:T(8,128)(2,1)S(1)} %get-tuple-element.28), channel_id=1, source_target_pairs={{0,3},{1,2},{2,1},{3,0},{4,7},{5,6},{6,5},{7,4},{8,11},{9,10},{10,... | collective-permute-start | bytes 233480 | tf_op jit(solution)/shard_map/ppermute | solution.py:25
  23.5 6.9 %collective-permute-start.8 = (bf16[304,128]{1,0:T(8,128)(2,1)S(1)}, bf16[304,128]{1,0:T(8,128)(2,1)S(1)}, u32[]{:S(2)}, u32[]{:S(2)}) collective-permute-start(bf16[304,128]{1,0:T(8,128)(2,1)S(1)} %get-tuple-element.29), channel_id=1, source_target_pairs={{0,2},{1,3},{2,0},{3,1},{4,6},{5,7},{6,4},{7,5},{8,10},{9,11},{10,... | collective-permute-start | bytes 233480 | tf_op jit(solution)/shard_map/ppermute | solution.py:25
  26.8 4.4 %collective-permute-start.9 = (bf16[304,128]{1,0:T(8,128)(2,1)S(1)}, bf16[304,128]{1,0:T(8,128)(2,1)S(1)}, u32[]{:S(2)}, u32[]{:S(2)}) collective-permute-start(bf16[304,128]{1,0:T(8,128)(2,1)S(1)} %get-tuple-element.30), channel_id=1, source_target_pairs={{0,1},{1,0},{2,3},{3,2},{4,5},{5,4},{6,7},{7,6},{8,9},{9,8},{10,11... | collective-permute-start | bytes 233480 | tf_op jit(solution)/shard_map/ppermute | solution.py:25
  31.9 9.5 %collective-permute-start.10 = (bf16[288,128]{1,0:T(8,128)(2,1)S(1)}, bf16[288,128]{1,0:T(8,128)(2,1)S(1)}, u32[]{:S(2)}, u32[]{:S(2)}) collective-permute-start(bf16[288,128]{1,0:T(8,128)(2,1)S(1)} %get-tuple-element.32), channel_id=1, source_target_pairs={{0,6},{1,7},{2,4},{3,5},{4,2},{5,3},{6,0},{7,1},{8,14},{9,15},{10,... | collective-permute-start | bytes 221192 | tf_op jit(solution)/shard_map/ppermute | solution.py:25
  34.7 9.5 %collective-permute-start.11 = (bf16[288,128]{1,0:T(8,128)(2,1)S(1)}, bf16[288,128]{1,0:T(8,128)(2,1)S(1)}, u32[]{:S(2)}, u32[]{:S(2)}) collective-permute-start(bf16[288,128]{1,0:T(8,128)(2,1)S(1)} %get-tuple-element.33), channel_id=1, source_target_pairs={{0,4},{1,5},{2,6},{3,7},{4,0},{5,1},{6,2},{7,3},{8,12},{9,13},{10,... | collective-permute-start | bytes 221192 | tf_op jit(solution)/shard_map/ppermute | solution.py:25
  34.7 10.4 %collective-permute-start.12 = (bf16[288,128]{1,0:T(8,128)(2,1)S(1)}, bf16[288,128]{1,0:T(8,128)(2,1)S(1)}, u32[]{:S(2)}, u32[]{:S(2)}) collective-permute-start(bf16[288,128]{1,0:T(8,128)(2,1)S(1)} %get-tuple-element.34), channel_id=1, source_target_pairs={{0,7},{1,6},{2,5},{3,4},{4,3},{5,2},{6,1},{7,0},{8,15},{9,14},{10,... | collective-permute-start | bytes 221192 | tf_op jit(solution)/shard_map/ppermute | solution.py:25
  36.7 10.6 %collective-permute-start.13 = (bf16[288,128]{1,0:T(8,128)(2,1)S(1)}, bf16[288,128]{1,0:T(8,128)(2,1)S(1)}, u32[]{:S(2)}, u32[]{:S(2)}) collective-permute-start(bf16[288,128]{1,0:T(8,128)(2,1)S(1)} %get-tuple-element.35), channel_id=1, source_target_pairs={{0,5},{1,4},{2,7},{3,6},{4,1},{5,0},{6,3},{7,2},{8,13},{9,12},{10,... | collective-permute-start | bytes 221192 | tf_op jit(solution)/shard_map/ppermute | solution.py:25
  39.1 8.3 %collective-permute-start.14 = (bf16[288,128]{1,0:T(8,128)(2,1)S(1)}, bf16[288,128]{1,0:T(8,128)(2,1)S(1)}, u32[]{:S(2)}, u32[]{:S(2)}) collective-permute-start(bf16[288,128]{1,0:T(8,128)(2,1)S(1)} %get-tuple-element.36), channel_id=1, source_target_pairs={{0,3},{1,2},{2,1},{3,0},{4,7},{5,6},{6,5},{7,4},{8,11},{9,10},{10,... | collective-permute-start | bytes 221192 | tf_op jit(solution)/shard_map/ppermute | solution.py:25
  41.4 5.9 %collective-permute-start.15 = (bf16[288,128]{1,0:T(8,128)(2,1)S(1)}, bf16[288,128]{1,0:T(8,128)(2,1)S(1)}, u32[]{:S(2)}, u32[]{:S(2)}) collective-permute-start(bf16[288,128]{1,0:T(8,128)(2,1)S(1)} %get-tuple-element.37), channel_id=1, source_target_pairs={{0,2},{1,3},{2,0},{3,1},{4,6},{5,7},{6,4},{7,5},{8,10},{9,11},{10,... | collective-permute-start | bytes 221192 | tf_op jit(solution)/shard_map/ppermute | solution.py:25
  44.1 4.4 %collective-permute-start.16 = (bf16[288,128]{1,0:T(8,128)(2,1)S(1)}, bf16[288,128]{1,0:T(8,128)(2,1)S(1)}, u32[]{:S(2)}, u32[]{:S(2)}) collective-permute-start(bf16[288,128]{1,0:T(8,128)(2,1)S(1)} %get-tuple-element.38), channel_id=1, source_target_pairs={{0,1},{1,0},{2,3},{3,2},{4,5},{5,4},{6,7},{7,6},{8,9},{9,8},{10,11... | collective-permute-start | bytes 221192 | tf_op jit(solution)/shard_map/ppermute | solution.py:25
  49.1 1.5 %collective-permute-start.17 = (bf16[2,2,6,32,128]{4,3,2,1,0:T(8,128)(2,1)S(1)}, bf16[2,2,6,32,128]{4,3,2,1,0:T(8,128)(2,1)S(1)}, u32[]{:S(2)}, u32[]{:S(2)}) collective-permute-start(bf16[2,2,6,32,128]{4,3,2,1,0:T(8,128)(2,1)S(1)} %get-tuple-element.42), channel_id=1, source_target_pairs={{0,8},{8,0},{16,24},{24,16},{1,9},{9,1},{17,25},{25,17},{2,10},{10... | collective-permute-start | bytes 589832 | tf_op jit(solution)/shard_map/ppermute | solution.py:188
  50.7 4.9 %collective-permute-start.18 = (bf16[2,6,32,128]{3,2,1,0:T(8,128)(2,1)S(1)}, bf16[2,6,32,128]{3,2,1,0:T(8,128)(2,1)S(1)}, u32[]{:S(2)}, u32[]{:S(2)}) collective-permute-start(bf16[2,6,32,128]{3,2,1,0:T(8,128)(2,1)S(1)} %fusion.1), channel_id=1, source_target_pairs={{0,16},{8,24},{16,0},{24,8},{1,17},{9,25},{17,1},{25,9},{2,18},{10... | collective-permute-start | bytes 294920 | tf_op jit(solution)/shard_map/ppermute | solution.py:190

commit v4 on v3

--- a/solution.py
+++ b/solution.py
@@ -15,9 +15,9 @@
 HBM = pl.BlockSpec(memory_space=pltpu.HBM)
 
 
-def far_first(n):
-    far, near = range(n // 2, n), range(n // 2 - 1, 0, -1)
-    return (0, *sorted(far, key=lambda k: (k & 1, -k)), *near)
+def start_order(n):
+    far = sorted(range(n // 2, n), key=lambda k: (k & 1, -k))
+    return (0, far[0], 1, *far[1:], *range(2, n // 2))
 
 
 def all_swapped(parts, steps, axis):
@@ -168,7 +168,7 @@
     shape = lambda *dims: jax.ShapeDtypeStruct(dims, jnp.bfloat16)
     scratch = lambda *dims: [pltpu.VMEM(dims, jnp.bfloat16)]
     bind = functools.partial
-    steps = far_first(n)
+    steps = start_order(n)
     here = jnp.stack([lax.axis_index("blk"), lax.axis_index("site")]).astype(jnp.int32)
     pieces = [shape(3 * slots * rows + TILE, m)] * n
     kept = scratch(3 * slots, m, m)

time: 56.5 us -> 55.2 us (0.977)
  starting transfers between devices: 28.7 us -> 28 us
  waiting for transfers between devices: 16.2 us -> 15.6 us
    ppermute x14, waiting for transfers between devices: 11.7 us -> 11 us  [all_swapped(): lax.ppermute(part, axis, [(i, i ^ k) for i in range(n)])]
    ppermute x14, starting transfers between devices: 22.5 us -> 21.9 us  [all_swapped(): lax.ppermute(part, axis, [(i, i ^ k) for i in range(n)])]
where the time goes in v4:
time: 55.2 us; the launch traced here: 55 us
  starting transfers between devices  28 us (51%)
  waiting for transfers between devices  15.6 us (28%)
  Pallas kernels  9 us (16%)
  between operations  1.52 us (3%)
  other arithmetic  0.9 us (2%)
    ppermute x14, starting transfers between devices, all_swapped(): lax.ppermute(part, axis, [(i, i ^ k) for i in range(n)])  21.9 us
    ppermute x14, waiting for transfers between devices, all_swapped(): lax.ppermute(part, axis, [(i, i ^ k) for i in range(n)])  11 us
    pallas_call x1, Pallas kernels, edge_proj(): pl.pallas_call(edge_proj_kernel, out_shape=jax.ShapeDtypeStruct((2 * slot...  5.28 us
    ppermute x1, starting transfers between devices, per_device(): lax.ppermute(left_corner, 'site', [(i, i if i % 2 else (i + 2) % sites) f...  4.78 us
    ppermute x1, waiting for transfers between devices, routed_by_tiles(): lax.ppermute(partial[1].astype(jnp.bfloat16), 'site', [(i, i ^ 2) for i i...  2.85 us
    ppermute x1, waiting for transfers between devices, routed_by_tiles(): came = lax.ppermute(away, 'site', [(i, i ^ 1) for i in range(sites)])  1.43 us
    pallas_call x1, Pallas kernels, routed_by_tiles(): small_call(bind(join_kernel, steps), pieces, ins, [], 'join')(here, *parts)  1.42 us
  transfers between devices with their start and end apart: 19, of which 9 were waited for; matrix products, arithmetic and copies ran while one was open for 0% of the time, Pallas kernels for 12%

profile of v4, /device:TPU:0, one launch (start us, length us, event | category | flops | bytes accessed | tf_op | source)
XLA Modules:
  0.0 55.0 jit_solution(5522944368066192454)
XLA Ops:
  0.6 0.5 collective-permute-start
  1.1 0.1 collective-permute-start.2
  2.0 0.1 pad_add_fusion.here
  2.1 0.0 copy-start
  2.1 0.3 collective-permute-done
  2.4 4.8 %collective-permute-start.1 = (bf16[1,6,128,128]{3,2,1,0:T(8,128)(2,1)S(1)}, bf16[1,6,128,128]{3,2,1,0:T(8,128)(2,1)S(1)}, u32[]{:S(2)}, u32[]{:S(2)}) collective-permute-start(bf16[1,6,128,128]{3,2,1,0:T(8,128)(2,1)S(1)} %collective-permute-done), channel_id=1, source_target_pairs={{0,16},{8,8},{16,0},{24,24},{1,17},{9,9},{17,1},{25,25},{2,18},{10... | collective-permute-start | bytes 589832 | tf_op jit(solution)/shard_map/ppermute | solution.py:226
  7.2 5.3 %edge_proj.1.wv = bf16[12,128,128]{2,1,0:T(8,128)(2,1)S(1)} custom-call(bf16[1,6,128,2304]{3,2,1,0:T(8,128)(2,1)} %edge.1, bf16[1,6,128,2304]{3,2,1,0:T(8,128)(2,1)} %bedge.1, bf16[1,6,2304,128]{3,2,1,0:T(8,128)(2,1)} %proj.1), custom_call_target="tpu_custom_call" | custom-call | flops 905969664 | bytes 10616832 | tf_op jit(solution)/shard_map/edge_proj/pallas_call | solution.py:52
  12.5 0.1 pad_maximum_fusion.turn
  12.6 0.0 collective-permute-done.1.corner
  12.6 0.0 collective-permute-done.2.bcorner
  12.6 1.0 %spread.1 = (bf16[304,128]{1,0:T(8,128)(2,1)S(1)}, bf16[304,128]{1,0:T(8,128)(2,1)S(1)}, bf16[304,128]{1,0:T(8,128)(2,1)S(1)}, bf16[304,128]{1,0:T(8,128)(2,1)S(...) custom-call(s32[2]{0:T(128)S(1)} %pad_add_fusion.here, ...), custom_call_target="tpu_custom_call" | custom-call | flops 268435456 | bytes 1048576 | tf_op jit(solution)/shard_map/spread/pallas_call | solution.py:175
  13.6 3.7 %collective-permute-start.3 = (bf16[304,128]{1,0:T(8,128)(2,1)S(1)}, bf16[304,128]{1,0:T(8,128)(2,1)S(1)}, u32[]{:S(2)}, u32[]{:S(2)}) collective-permute-start(bf16[304,128]{1,0:T(8,128)(2,1)S(1)} %get-tuple-element.24), channel_id=1, source_target_pairs={{0,6},{1,7},{2,4},{3,5},{4,2},{5,3},{6,0},{7,1},{8,14},{9,15},{10,... | collective-permute-start | bytes 233480 | tf_op jit(solution)/shard_map/ppermute | solution.py:25
  17.3 1.5 %collective-permute-start.4 = (bf16[304,128]{1,0:T(8,128)(2,1)S(1)}, bf16[304,128]{1,0:T(8,128)(2,1)S(1)}, u32[]{:S(2)}, u32[]{:S(2)}) collective-permute-start(bf16[304,128]{1,0:T(8,128)(2,1)S(1)} %get-tuple-element.25), channel_id=1, source_target_pairs={{0,1},{1,0},{2,3},{3,2},{4,5},{5,4},{6,7},{7,6},{8,9},{9,8},{10,11... | collective-permute-start | bytes 233480 | tf_op jit(solution)/shard_map/ppermute | solution.py:25
  18.8 0.0 collective-permute-start.5
  18.8 1.9 %collective-permute-start.6 = (bf16[304,128]{1,0:T(8,128)(2,1)S(1)}, bf16[304,128]{1,0:T(8,128)(2,1)S(1)}, u32[]{:S(2)}, u32[]{:S(2)}) collective-permute-start(bf16[304,128]{1,0:T(8,128)(2,1)S(1)} %get-tuple-element.27), channel_id=1, source_target_pairs={{0,7},{1,6},{2,5},{3,4},{4,3},{5,2},{6,1},{7,0},{8,15},{9,14},{10,... | collective-permute-start | bytes 233480 | tf_op jit(solution)/shard_map/ppermute | solution.py:25
  20.7 1.3 %collective-permute-start.7 = (bf16[304,128]{1,0:T(8,128)(2,1)S(1)}, bf16[304,128]{1,0:T(8,128)(2,1)S(1)}, u32[]{:S(2)}, u32[]{:S(2)}) collective-permute-start(bf16[304,128]{1,0:T(8,128)(2,1)S(1)} %get-tuple-element.28), channel_id=1, source_target_pairs={{0,5},{1,4},{2,7},{3,6},{4,1},{5,0},{6,3},{7,2},{8,13},{9,12},{10,... | collective-permute-start | bytes 233480 | tf_op jit(solution)/shard_map/ppermute | solution.py:25
  21.9 0.0 collective-permute-done.3.refs_1_
  21.9 2.4 %collective-permute-start.8 = (bf16[304,128]{1,0:T(8,128)(2,1)S(1)}, bf16[304,128]{1,0:T(8,128)(2,1)S(1)}, u32[]{:S(2)}, u32[]{:S(2)}) collective-permute-start(bf16[304,128]{1,0:T(8,128)(2,1)S(1)} %get-tuple-element.29), channel_id=1, source_target_pairs={{0,2},{1,3},{2,0},{3,1},{4,6},{5,7},{6,4},{7,5},{8,10},{9,11},{10,... | collective-permute-start | bytes 233480 | tf_op jit(solution)/shard_map/ppermute | solution.py:25
  24.3 0.0 collective-permute-done.4.refs_2_
  24.3 0.9 %collective-permute-start.9 = (bf16[304,128]{1,0:T(8,128)(2,1)S(1)}, bf16[304,128]{1,0:T(8,128)(2,1)S(1)}, u32[]{:S(2)}, u32[]{:S(2)}) collective-permute-start(bf16[304,128]{1,0:T(8,128)(2,1)S(1)} %get-tuple-element.30), channel_id=1, source_target_pairs={{0,3},{1,2},{2,1},{3,0},{4,7},{5,6},{6,5},{7,4},{8,11},{9,10},{10,... | collective-permute-start | bytes 233480 | tf_op jit(solution)/shard_map/ppermute | solution.py:25
  25.2 1.4 %collective-permute-done.5.refs_3_ = bf16[304,128]{1,0:T(8,128)(2,1)S(1)} collective-permute-done((bf16[304,128]{1,0:T(8,128)(2,1)S(1)}, bf16[304,128]{1,0:T(8,128)(2,1)S(1)}, u32[]{:S(2)}, u32[]{:S(2)}) %collective-permute-start.5) | collective-permute-done | bytes 77856 | tf_op jit(solution)/shard_map/ppermute | solution.py:25
  26.6 0.0 collective-permute-done.6.refs_4_
  26.6 4.1 %collective-permute-done.7.refs_5_ = bf16[304,128]{1,0:T(8,128)(2,1)S(1)} collective-permute-done((bf16[304,128]{1,0:T(8,128)(2,1)S(1)}, bf16[304,128]{1,0:T(8,128)(2,1)S(1)}, u32[]{:S(2)}, u32[]{:S(2)}) %collective-permute-start.7) | collective-permute-done | bytes 77856 | tf_op jit(solution)/shard_map/ppermute | solution.py:25
  30.8 0.0 collective-permute-done.8.refs_6_
  30.8 0.3 collective-permute-done.9.refs_7_
  31.1 0.0 copy-done
  31.1 0.7 %route.1 = (bf16[288,128]{1,0:T(8,128)(2,1)S(1)}, bf16[288,128]{1,0:T(8,128)(2,1)S(1)}, bf16[288,128]{1,0:T(8,128)(2,1)S(1)}, bf16[288,128]{1,0:T(8,128)(2,1)S(1...) custom-call(s32[2]{0:T(128)S(1)} %pad_add_fusion.here, ...), custom_call_target="tpu_custom_call" | custom-call | flops 268435456 | bytes 1048576 | tf_op jit(solution)/shard_map/route/pallas_call | solution.py:181
  31.8 2.7 %collective-permute-start.10 = (bf16[288,128]{1,0:T(8,128)(2,1)S(1)}, bf16[288,128]{1,0:T(8,128)(2,1)S(1)}, u32[]{:S(2)}, u32[]{:S(2)}) collective-permute-start(bf16[288,128]{1,0:T(8,128)(2,1)S(1)} %get-tuple-element.32), channel_id=1, source_target_pairs={{0,6},{1,7},{2,4},{3,5},{4,2},{5,3},{6,0},{7,1},{8,14},{9,15},{10,... | collective-permute-start | bytes 221192 | tf_op jit(solution)/shard_map/ppermute | solution.py:25
  34.5 1.0 %collective-permute-start.11 = (bf16[288,128]{1,0:T(8,128)(2,1)S(1)}, bf16[288,128]{1,0:T(8,128)(2,1)S(1)}, u32[]{:S(2)}, u32[]{:S(2)}) collective-permute-start(bf16[288,128]{1,0:T(8,128)(2,1)S(1)} %get-tuple-element.33), channel_id=1, source_target_pairs={{0,1},{1,0},{2,3},{3,2},{4,5},{5,4},{6,7},{7,6},{8,9},{9,8},{10,11... | collective-permute-start | bytes 221192 | tf_op jit(solution)/shard_map/ppermute | solution.py:25
  35.4 0.0 collective-permute-start.12
  35.4 1.7 %collective-permute-start.13 = (bf16[288,128]{1,0:T(8,128)(2,1)S(1)}, bf16[288,128]{1,0:T(8,128)(2,1)S(1)}, u32[]{:S(2)}, u32[]{:S(2)}) collective-permute-start(bf16[288,128]{1,0:T(8,128)(2,1)S(1)} %get-tuple-element.35), channel_id=1, source_target_pairs={{0,7},{1,6},{2,5},{3,4},{4,3},{5,2},{6,1},{7,0},{8,15},{9,14},{10,... | collective-permute-start | bytes 221192 | tf_op jit(solution)/shard_map/ppermute | solution.py:25
  37.1 2.4 %collective-permute-start.14 = (bf16[288,128]{1,0:T(8,128)(2,1)S(1)}, bf16[288,128]{1,0:T(8,128)(2,1)S(1)}, u32[]{:S(2)}, u32[]{:S(2)}) collective-permute-start(bf16[288,128]{1,0:T(8,128)(2,1)S(1)} %get-tuple-element.36), channel_id=1, source_target_pairs={{0,5},{1,4},{2,7},{3,6},{4,1},{5,0},{6,3},{7,2},{8,13},{9,12},{10,... | collective-permute-start | bytes 221192 | tf_op jit(solution)/shard_map/ppermute | solution.py:25
  39.6 0.0 collective-permute-done.10.refs_1_
  39.6 1.1 %collective-permute-start.15 = (bf16[288,128]{1,0:T(8,128)(2,1)S(1)}, bf16[288,128]{1,0:T(8,128)(2,1)S(1)}, u32[]{:S(2)}, u32[]{:S(2)}) collective-permute-start(bf16[288,128]{1,0:T(8,128)(2,1)S(1)} %get-tuple-element.37), channel_id=1, source_target_pairs={{0,2},{1,3},{2,0},{3,1},{4,6},{5,7},{6,4},{7,5},{8,10},{9,11},{10,... | collective-permute-start | bytes 221192 | tf_op jit(solution)/shard_map/ppermute | solution.py:25
  40.7 0.0 collective-permute-done.11.refs_2_
  40.7 1.4 %collective-permute-start.16 = (bf16[288,128]{1,0:T(8,128)(2,1)S(1)}, bf16[288,128]{1,0:T(8,128)(2,1)S(1)}, u32[]{:S(2)}, u32[]{:S(2)}) collective-permute-start(bf16[288,128]{1,0:T(8,128)(2,1)S(1)} %get-tuple-element.38), channel_id=1, source_target_pairs={{0,3},{1,2},{2,1},{3,0},{4,7},{5,6},{6,5},{7,4},{8,11},{9,10},{10,... | collective-permute-start | bytes 221192 | tf_op jit(solution)/shard_map/ppermute | solution.py:25
  42.1 1.0 %collective-permute-done.12.refs_3_ = bf16[288,128]{1,0:T(8,128)(2,1)S(1)} collective-permute-done((bf16[288,128]{1,0:T(8,128)(2,1)S(1)}, bf16[288,128]{1,0:T(8,128)(2,1)S(1)}, u32[]{:S(2)}, u32[]{:S(2)}) %collective-permute-start.12) | collective-permute-done | bytes 73760 | tf_op jit(solution)/shard_map/ppermute | solution.py:25
  43.1 0.0 collective-permute-done.13.refs_4_
  43.1 3.7 %collective-permute-done.14.refs_5_ = bf16[288,128]{1,0:T(8,128)(2,1)S(1)} collective-permute-done((bf16[288,128]{1,0:T(8,128)(2,1)S(1)}, bf16[288,128]{1,0:T(8,128)(2,1)S(1)}, u32[]{:S(2)}, u32[]{:S(2)}) %collective-permute-start.14) | collective-permute-done | bytes 73760 | tf_op jit(solution)/shard_map/ppermute | solution.py:25
  46.9 0.0 collective-permute-done.15.refs_6_
  46.9 0.4 collective-permute-done.16.refs_7_
  47.2 0.6 %share.1 = (bf16[2,2,6,32,128]{4,3,2,1,0:T(8,128)(2,1)S(1)}, bf16[2,2,6,32,128]{4,3,2,1,0:T(8,128)(2,1)S(1)}) custom-call(s32[2]{0:T(128)S(1)} %pad_add_fusion.here, bf16[288,128]{1,0:T(8,128)(2,1)S(1)} %get-tuple-element.31.refs_0_, bf16[288,128]{1,0:T(8,128)(2,1)S(1)} %collective-permute-done.10.refs_1_, ...), custom_call_target="tpu_custom_call" | custom-call | flops 268435456 | bytes 1048576 | tf_op jit(solution)/shard_map/share/pallas_call | solution.py:187
  47.8 0.1 collective-permute-start.17
  47.9 1.4 %collective-permute-done.17 = bf16[2,2,6,32,128]{4,3,2,1,0:T(8,128)(2,1)S(1)} collective-permute-done((bf16[2,2,6,32,128]{4,3,2,1,0:T(8,128)(2,1)S(1)}, bf16[2,2,6,32,128]{4,3,2,1,0:T(8,128)(2,1)S(1)}, u32[]{:S(2)}, u32[]{:S(2)}) %collective-permute-start.17) | collective-permute-done | bytes 196640 | tf_op jit(solution)/shard_map/ppermute | solution.py:188
  49.4 0.6 %collective-permute-start.18 = (bf16[2,6,32,128]{3,2,1,0:T(8,128)(2,1)S(1)}, bf16[2,6,32,128]{3,2,1,0:T(8,128)(2,1)S(1)}, u32[]{:S(2)}, u32[]{:S(2)}) collective-permute-start(bf16[2,6,32,128]{3,2,1,0:T(8,128)(2,1)S(1)} %fusion.1), channel_id=1, source_target_pairs={{0,16},{8,24},{16,0},{24,8},{1,17},{9,25},{17,1},{25,9},{2,18},{10... | collective-permute-start | bytes 294920 | tf_op jit(solution)/shard_map/ppermute | solution.py:190
  50.1 1.4 %join.1 = (bf16[1,6,128,128]{3,2,1,0:T(8,128)(2,1)}, bf16[2,1,6,128,128]{4,3,2,1,0:T(8,128)(2,1)}) custom-call(s32[2]{0:T(128)S(1)} %pad_add_fusion.here, bf16[288,128]{1,0:T(8,128)(2,1)S(1)} %get-tuple-element.31.refs_0_, bf16[288,128]{1,0:T(8,128)(2,1)S(1)} %collective-permute-done.10.refs_1_, bf16[288,128]{1,0:T(8,128)(2,1)S(1)} %collective-permute-done.11.refs_2_, ...), custom_call_target="tpu_custom_call" | custom-call | flops 268435456 | bytes 1048576 | tf_op jit(solution)/shard_map/join/pallas_call | solution.py:192
  51.5 2.8 %collective-permute-done.18 = bf16[2,6,32,128]{3,2,1,0:T(8,128)(2,1)S(1)} collective-permute-done((bf16[2,6,32,128]{3,2,1,0:T(8,128)(2,1)S(1)}, bf16[2,6,32,128]{3,2,1,0:T(8,128)(2,1)S(1)}, u32[]{:S(2)}, u32[]{:S(2)}) %collective-permute-start.18) | collective-permute-done | bytes 98336 | tf_op jit(solution)/shard_map/ppermute | solution.py:190
  54.3 0.7 %fusion = f32[2,6,32,128]{3,2,1,0:T(8,128)} fusion(f32[2,2,6,32,128]{4,3,2,1,0:T(8,128)S(1)} %convert_add_fusion, bf16[2,6,32,128]{3,2,1,0:T(8,128)(2,1)S(1)} %collective-permute-done.18), kind=kLoop, calls=%fused_computation.3 | loop fusion | flops 98304 | bytes 491520 | tf_op jit(solution)/shard_map/add | solution.py:193
  (2 shorter events, 0.1 us)
Async XLA Ops:
  0.6 1.8 %collective-permute-start = (bf16[1,6,128,128]{3,2,1,0:T(8,128)(2,1)}, bf16[1,6,128,128]{3,2,1,0:T(8,128)(2,1)S(1)}, u32[]{:S(2)}, u32[]{:S(2)}) collective-permute-start(bf16[1,6,128,128]{3,2,1,0:T(8,128)(2,1)} %param.7), channel_id=1, source_target_pairs={{0,8},{8,0},{16,24},{24,16},{1,9},{9,1},{17,25},{25,17},{2,10},{10... | collective-permute-start | bytes 589832 | tf_op jit(solution)/shard_map/ppermute | solution.py:225
  1.1 11.4 %collective-permute-start.2 = (bf16[2,1,6,128,128]{4,3,2,1,0:T(8,128)(2,1)}, bf16[2,1,6,128,128]{4,3,2,1,0:T(8,128)(2,1)S(1)}, u32[]{:S(2)}, u32[]{:S(2)}) collective-permute-start(bf16[2,1,6,128,128]{4,3,2,1,0:T(8,128)(2,1)} %param.8), channel_id=1, source_target_pairs={{0,8},{8,16},{16,24},{24,0},{1,9},{9,17},{17,25},{25,1},{2,10},{10... | collective-permute-start | bytes 1179656 | tf_op jit(solution)/shard_map/ppermute | solution.py:224
  2.1 29.0 %copy-start = (s32[1,48]{1,0:T(1,128)S(1)}, s32[1,48]{1,0:T(1,128)}, u32[]{:S(2)}) copy-start(s32[1,48]{1,0:T(1,128)} %joining.1) | copy-start | bytes 580
  2.4 10.2 %collective-permute-start.1 = (bf16[1,6,128,128]{3,2,1,0:T(8,128)(2,1)S(1)}, bf16[1,6,128,128]{3,2,1,0:T(8,128)(2,1)S(1)}, u32[]{:S(2)}, u32[]{:S(2)}) collective-permute-start(bf16[1,6,128,128]{3,2,1,0:T(8,128)(2,1)S(1)} %collective-permute-done), channel_id=1, source_target_pairs={{0,16},{8,8},{16,0},{24,24},{1,17},{9,9},{17,1},{25,25},{2,18},{10... | collective-permute-start | bytes 589832 | tf_op jit(solution)/shard_map/ppermute | solution.py:226
  13.6 8.3 %collective-permute-start.3 = (bf16[304,128]{1,0:T(8,128)(2,1)S(1)}, bf16[304,128]{1,0:T(8,128)(2,1)S(1)}, u32[]{:S(2)}, u32[]{:S(2)}) collective-permute-start(bf16[304,128]{1,0:T(8,128)(2,1)S(1)} %get-tuple-element.24), channel_id=1, source_target_pairs={{0,6},{1,7},{2,4},{3,5},{4,2},{5,3},{6,0},{7,1},{8,14},{9,15},{10,... | collective-permute-start | bytes 233480 | tf_op jit(solution)/shard_map/ppermute | solution.py:25
  17.3 7.0 %collective-permute-start.4 = (bf16[304,128]{1,0:T(8,128)(2,1)S(1)}, bf16[304,128]{1,0:T(8,128)(2,1)S(1)}, u32[]{:S(2)}, u32[]{:S(2)}) collective-permute-start(bf16[304,128]{1,0:T(8,128)(2,1)S(1)} %get-tuple-element.25), channel_id=1, source_target_pairs={{0,1},{1,0},{2,3},{3,2},{4,5},{5,4},{6,7},{7,6},{8,9},{9,8},{10,11... | collective-permute-start | bytes 233480 | tf_op jit(solution)/shard_map/ppermute | solution.py:25
  18.8 7.9 %collective-permute-start.5 = (bf16[304,128]{1,0:T(8,128)(2,1)S(1)}, bf16[304,128]{1,0:T(8,128)(2,1)S(1)}, u32[]{:S(2)}, u32[]{:S(2)}) collective-permute-start(bf16[304,128]{1,0:T(8,128)(2,1)S(1)} %get-tuple-element.26), channel_id=1, source_target_pairs={{0,4},{1,5},{2,6},{3,7},{4,0},{5,1},{6,2},{7,3},{8,12},{9,13},{10,... | collective-permute-start | bytes 233480 | tf_op jit(solution)/shard_map/ppermute | solution.py:25
  18.8 7.9 %collective-permute-start.6 = (bf16[304,128]{1,0:T(8,128)(2,1)S(1)}, bf16[304,128]{1,0:T(8,128)(2,1)S(1)}, u32[]{:S(2)}, u32[]{:S(2)}) collective-permute-start(bf16[304,128]{1,0:T(8,128)(2,1)S(1)} %get-tuple-element.27), channel_id=1, source_target_pairs={{0,7},{1,6},{2,5},{3,4},{4,3},{5,2},{6,1},{7,0},{8,15},{9,14},{10,... | collective-permute-start | bytes 233480 | tf_op jit(solution)/shard_map/ppermute | solution.py:25
  20.7 10.1 %collective-permute-start.7 = (bf16[304,128]{1,0:T(8,128)(2,1)S(1)}, bf16[304,128]{1,0:T(8,128)(2,1)S(1)}, u32[]{:S(2)}, u32[]{:S(2)}) collective-permute-start(bf16[304,128]{1,0:T(8,128)(2,1)S(1)} %get-tuple-element.28), channel_id=1, source_target_pairs={{0,5},{1,4},{2,7},{3,6},{4,1},{5,0},{6,3},{7,2},{8,13},{9,12},{10,... | collective-permute-start | bytes 233480 | tf_op jit(solution)/shard_map/ppermute | solution.py:25
  21.9 8.8 %collective-permute-start.8 = (bf16[304,128]{1,0:T(8,128)(2,1)S(1)}, bf16[304,128]{1,0:T(8,128)(2,1)S(1)}, u32[]{:S(2)}, u32[]{:S(2)}) collective-permute-start(bf16[304,128]{1,0:T(8,128)(2,1)S(1)} %get-tuple-element.29), channel_id=1, source_target_pairs={{0,2},{1,3},{2,0},{3,1},{4,6},{5,7},{6,4},{7,5},{8,10},{9,11},{10,... | collective-permute-start | bytes 233480 | tf_op jit(solution)/shard_map/ppermute | solution.py:25
  24.3 6.7 %collective-permute-start.9 = (bf16[304,128]{1,0:T(8,128)(2,1)S(1)}, bf16[304,128]{1,0:T(8,128)(2,1)S(1)}, u32[]{:S(2)}, u32[]{:S(2)}) collective-permute-start(bf16[304,128]{1,0:T(8,128)(2,1)S(1)} %get-tuple-element.30), channel_id=1, source_target_pairs={{0,3},{1,2},{2,1},{3,0},{4,7},{5,6},{6,5},{7,4},{8,11},{9,10},{10,... | collective-permute-start | bytes 233480 | tf_op jit(solution)/shard_map/ppermute | solution.py:25
  31.8 7.8 %collective-permute-start.10 = (bf16[288,128]{1,0:T(8,128)(2,1)S(1)}, bf16[288,128]{1,0:T(8,128)(2,1)S(1)}, u32[]{:S(2)}, u32[]{:S(2)}) collective-permute-start(bf16[288,128]{1,0:T(8,128)(2,1)S(1)} %get-tuple-element.32), channel_id=1, source_target_pairs={{0,6},{1,7},{2,4},{3,5},{4,2},{5,3},{6,0},{7,1},{8,14},{9,15},{10,... | collective-permute-start | bytes 221192 | tf_op jit(solution)/shard_map/ppermute | solution.py:25
  34.5 6.3 %collective-permute-start.11 = (bf16[288,128]{1,0:T(8,128)(2,1)S(1)}, bf16[288,128]{1,0:T(8,128)(2,1)S(1)}, u32[]{:S(2)}, u32[]{:S(2)}) collective-permute-start(bf16[288,128]{1,0:T(8,128)(2,1)S(1)} %get-tuple-element.33), channel_id=1, source_target_pairs={{0,1},{1,0},{2,3},{3,2},{4,5},{5,4},{6,7},{7,6},{8,9},{9,8},{10,11... | collective-permute-start | bytes 221192 | tf_op jit(solution)/shard_map/ppermute | solution.py:25
  35.4 7.7 %collective-permute-start.12 = (bf16[288,128]{1,0:T(8,128)(2,1)S(1)}, bf16[288,128]{1,0:T(8,128)(2,1)S(1)}, u32[]{:S(2)}, u32[]{:S(2)}) collective-permute-start(bf16[288,128]{1,0:T(8,128)(2,1)S(1)} %get-tuple-element.34), channel_id=1, source_target_pairs={{0,4},{1,5},{2,6},{3,7},{4,0},{5,1},{6,2},{7,3},{8,12},{9,13},{10,... | collective-permute-start | bytes 221192 | tf_op jit(solution)/shard_map/ppermute | solution.py:25
  35.4 7.7 %collective-permute-start.13 = (bf16[288,128]{1,0:T(8,128)(2,1)S(1)}, bf16[288,128]{1,0:T(8,128)(2,1)S(1)}, u32[]{:S(2)}, u32[]{:S(2)}) collective-permute-start(bf16[288,128]{1,0:T(8,128)(2,1)S(1)} %get-tuple-element.35), channel_id=1, source_target_pairs={{0,7},{1,6},{2,5},{3,4},{4,3},{5,2},{6,1},{7,0},{8,15},{9,14},{10,... | collective-permute-start | bytes 221192 | tf_op jit(solution)/shard_map/ppermute | solution.py:25
  37.1 9.7 %collective-permute-start.14 = (bf16[288,128]{1,0:T(8,128)(2,1)S(1)}, bf16[288,128]{1,0:T(8,128)(2,1)S(1)}, u32[]{:S(2)}, u32[]{:S(2)}) collective-permute-start(bf16[288,128]{1,0:T(8,128)(2,1)S(1)} %get-tuple-element.36), channel_id=1, source_target_pairs={{0,5},{1,4},{2,7},{3,6},{4,1},{5,0},{6,3},{7,2},{8,13},{9,12},{10,... | collective-permute-start | bytes 221192 | tf_op jit(solution)/shard_map/ppermute | solution.py:25
  39.6 7.3 %collective-permute-start.15 = (bf16[288,128]{1,0:T(8,128)(2,1)S(1)}, bf16[288,128]{1,0:T(8,128)(2,1)S(1)}, u32[]{:S(2)}, u32[]{:S(2)}) collective-permute-start(bf16[288,128]{1,0:T(8,128)(2,1)S(1)} %get-tuple-element.37), channel_id=1, source_target_pairs={{0,2},{1,3},{2,0},{3,1},{4,6},{5,7},{6,4},{7,5},{8,10},{9,11},{10,... | collective-permute-start | bytes 221192 | tf_op jit(solution)/shard_map/ppermute | solution.py:25
  40.7 6.5 %collective-permute-start.16 = (bf16[288,128]{1,0:T(8,128)(2,1)S(1)}, bf16[288,128]{1,0:T(8,128)(2,1)S(1)}, u32[]{:S(2)}, u32[]{:S(2)}) collective-permute-start(bf16[288,128]{1,0:T(8,128)(2,1)S(1)} %get-tuple-element.38), channel_id=1, source_target_pairs={{0,3},{1,2},{2,1},{3,0},{4,7},{5,6},{6,5},{7,4},{8,11},{9,10},{10,... | collective-permute-start | bytes 221192 | tf_op jit(solution)/shard_map/ppermute | solution.py:25
  47.8 1.5 %collective-permute-start.17 = (bf16[2,2,6,32,128]{4,3,2,1,0:T(8,128)(2,1)S(1)}, bf16[2,2,6,32,128]{4,3,2,1,0:T(8,128)(2,1)S(1)}, u32[]{:S(2)}, u32[]{:S(2)}) collective-permute-start(bf16[2,2,6,32,128]{4,3,2,1,0:T(8,128)(2,1)S(1)} %get-tuple-element.42), channel_id=1, source_target_pairs={{0,8},{8,0},{16,24},{24,16},{1,9},{9,1},{17,25},{25,17},{2,10},{10... | collective-permute-start | bytes 589832 | tf_op jit(solution)/shard_map/ppermute | solution.py:188
  49.4 4.9 %collective-permute-start.18 = (bf16[2,6,32,128]{3,2,1,0:T(8,128)(2,1)S(1)}, bf16[2,6,32,128]{3,2,1,0:T(8,128)(2,1)S(1)}, u32[]{:S(2)}, u32[]{:S(2)}) collective-permute-start(bf16[2,6,32,128]{3,2,1,0:T(8,128)(2,1)S(1)} %fusion.1), channel_id=1, source_target_pairs={{0,16},{8,24},{16,0},{24,8},{1,17},{9,25},{17,1},{25,9},{2,18},{10... | collective-permute-start | bytes 294920 | tf_op jit(solution)/shard_map/ppermute | solution.py:190
